TPU v7x, 256 devices: a whole 4x4x8 slice. The times are simulated.
256 devices in a mesh: seq: 8 (over y, x_hi), head: 32 (over z, x_lo, core).
Axes of the slice: x: 4 (x_hi: 2, x_lo: 2; x = x_hi * 2 + x_lo), y: 4, z: 8, core: 2. Of those that a mesh axis runs over, the one named last changes fastest.
Arguments:
- queries: bfloat16 [1024, 16384], P('seq', 'head'), may hold values from -15 to 15
- cache_keys: bfloat16 [8, 32, 1024, 128], P('seq', 'head'), may hold values from -4 to 4
- cache_values: bfloat16 [8, 32, 1024, 128], P('seq', 'head'), may hold values from -5 to 5
- new_keys: bfloat16 [1024, 1024], P('seq'), may hold values from -4 to 4
- new_values: bfloat16 [1024, 1024], P('seq'), may hold values from -5 to 5
- out_weight: bfloat16 [16384, 16384], P('head', 'seq'), may hold values from -0.0234375 to 0.0234375
- cache_lengths: int32 [8], replicated, may hold values from 1 to 4096, 16384 in all
- positions: int32 [1024], P('seq'), may hold values from 0 to 1023, each once
Outputs:
- mixed: bfloat16 [1024, 16384], P(('seq', 'head'))
Inputs may be any that keep to these rules, and one draw needn't show every extreme that they name: `cache_lengths`: live slots of each group; they add up to 16384 and one group is full. `positions`: each of 0 to 1023 once.
All inputs are finite; a program needn't handle non-finite values.
Results may differ from a plain program's by a relative error of at most 0.0095.
Values may be sent and summed in bfloat16 or wider, within the bound.
No kernel may reach another device: no remote copies, remote signals or barrier semaphores. Data moves between devices by JAX's collectives and lax.ppermute only.
A program may use at most 128 MiB of HBM per device.

v0:
```python
import math

import jax
import jax.numpy as jnp
from jax import lax
from jax.experimental import pallas as pl
from jax.experimental.pallas import tpu as pltpu
from jax.sharding import Mesh, PartitionSpec as P

HD = 128
HEADS = 4
TOK = 128
SLOTS = 1024
ROWS = 2048
HEAD_ROWS = 512
BLOCK = 1024
VROWS = HD + 16
NEG = -1e30
FRESH = 32
WIDE = 1024
TO_LOG2 = math.log2(math.e) / math.sqrt(HD)
F32 = jnp.float32
BF16 = jnp.bfloat16
VMEM = pl.BlockSpec(memory_space=pltpu.VMEM)
SMEM = pl.BlockSpec(memory_space=pltpu.SMEM)
HBM = pl.BlockSpec(memory_space=pltpu.HBM)


def moved(value, axis, size, step):
    return lax.ppermute(value, axis, [(i, (i + step) % size) for i in range(size)])


def along_y(value, step):
    return moved(value, ("yp", "yl"), 4, step)


def to_y_pair(value, flip):
    pairs = []
    for y in range(4):
        for core in range(2):
            other = y ^ 1 if core == flip else (y + (1 if y % 2 else 3)) % 4
            pairs.append((y * 2 + core, other * 2 + core))
    return lax.ppermute(value, ("yp", "yl", "core"), pairs)


def y_index():
    return lax.axis_index("yp") * 2 + lax.axis_index("yl")


def along_x(value, step):
    return moved(value, ("xh", "xl"), 4, step)


def along_z(value, step):
    return moved(value, "z", 8, step)


def to_other_core(value):
    return moved(value, "core", 2, 1)


def after(value, earlier):
    return lax.optimization_barrier((value, earlier))[0]


def params(mib):
    return pltpu.CompilerParams(vmem_limit_bytes=mib * 2**20)


def pack_body(q_hbm, k_hbm, v_hbm, nk_hbm, nv_hbm, pos_ref, q_out, kv_out, col_ref, sems):
    z = lax.axis_index("z")
    quarter = lax.axis_index("xl") * 2 + lax.axis_index("core")
    lanes = pl.ds(pl.multiple_of(z * HD, HD), HD)
    rows = pl.ds(pl.multiple_of(quarter * FRESH, FRESH), FRESH)
    start = 2 * SLOTS
    copies = [
        pltpu.make_async_copy(source, target, sems.at[i])
        for i, (source, target) in enumerate(
            (
                (q_hbm, q_out.at[pl.ds(0, TOK)]),
                (k_hbm, kv_out.at[pl.ds(0, SLOTS)]),
                (v_hbm, kv_out.at[pl.ds(SLOTS, SLOTS)]),
                (nk_hbm.at[rows, lanes], kv_out.at[pl.ds(start, FRESH)]),
                (nv_hbm.at[rows, lanes], kv_out.at[pl.ds(start + FRESH, FRESH)]),
            )
        )
    ]
    for copy in copies:
        copy.start()
    pos = jnp.broadcast_to(pos_ref[...].astype(F32), (TOK, TOK))
    high = jnp.floor(pos * (1.0 / 128.0))
    low = pos - high * 128.0
    q_out[TOK : TOK + 16, :] = jnp.zeros((16, HEADS * HD), BF16)
    row = lax.broadcasted_iota(jnp.int32, (16, TOK), 0)
    coded = jnp.where(row == 0, high[0:16], jnp.where(row == 1, low[0:16], 0.0))
    q_out[TOK : TOK + 16, 0:TOK] = coded.astype(BF16)
    col_ref[...] = high.T
    kv_out[start + 2 * FRESH : start + 3 * FRESH, :] = col_ref[rows, :].astype(BF16)
    col_ref[...] = low.T
    kv_out[start + 3 * FRESH : start + 4 * FRESH, :] = col_ref[rows, :].astype(BF16)
    for copy in copies:
        copy.wait()


def pack(queries, keys, values, new_keys, new_values, positions):
    return pl.pallas_call(
        pack_body,
        out_shape=[
            jax.ShapeDtypeStruct((TOK + 16, HEADS * HD), BF16),
            jax.ShapeDtypeStruct((2 * SLOTS + 4 * FRESH, HD), BF16),
        ],
        in_specs=[HBM] * 5 + [VMEM],
        out_specs=[VMEM] * 2,
        scratch_shapes=[pltpu.VMEM((TOK, TOK), F32), pltpu.SemaphoreType.DMA((5,))],
        name="pack",
    )(queries, keys, values, new_keys, new_values, positions)


def halves_body(w_hbm, w_kept, w_away, sems):
    core = lax.axis_index("core")
    copies = [
        pltpu.make_async_copy(
            w_hbm.at[:, pl.ds(pl.multiple_of(half * WIDE, WIDE), WIDE)], target, sems.at[i]
        )
        for i, (half, target) in enumerate(((core, w_kept), (1 - core, w_away)))
    ]
    for copy in copies:
        copy.start()
    for copy in copies:
        copy.wait()


def halves(weight):
    return pl.pallas_call(
        halves_body,
        out_shape=[jax.ShapeDtypeStruct((weight.shape[0], WIDE), BF16)] * 2,
        in_specs=[HBM],
        out_specs=[VMEM] * 2,
        scratch_shapes=[pltpu.SemaphoreType.DMA((2,))],
        name="halves",
    )(weight)


def update(s, values_t, cols, m_ref, acc_ref):
    old = m_ref[:, cols]
    new = jnp.maximum(old, jnp.max(s, axis=0, keepdims=True))
    p = jnp.exp2(s - new).astype(BF16)
    m_ref[:, cols] = new
    acc_ref[:, cols] = acc_ref[:, cols] * jnp.exp2(old - new) + jnp.dot(
        values_t, p, preferred_element_type=F32
    )


def flash(block_count, base_ref, keys2, values_t, rows_t, m_ref, acc_ref, s_ref):
    def place(step):
        cols = pl.multiple_of((step % HEADS) * HEAD_ROWS, HEAD_ROWS)
        base = pl.multiple_of(base_ref[step // HEADS], BLOCK)
        return pl.ds(base, BLOCK), pl.ds(cols, HEAD_ROWS)

    def score(step, slot):
        at, cols = place(step)
        s_ref[slot] = jnp.dot(keys2[at, :], rows_t[:, cols], preferred_element_type=F32)

    def settle(step, slot):
        at, cols = place(step)
        update(s_ref[slot], values_t[:, at], cols, m_ref, acc_ref)

    steps = block_count * HEADS

    @pl.when(steps > 0)
    def _():
        score(0, 0)

    @pl.loop(0, steps // 2)
    def _(i):
        score(2 * i + 1, 1)
        settle(2 * i, 0)
        score(jnp.minimum(2 * i + 2, steps - 1), 0)
        settle(2 * i + 1, 1)


def absorb_fresh(carry_ref, kv_refs, rows_t, row_pos, m_ref, acc_ref):
    def fresh(part):
        pieces = []
        for j in range(carry_ref.shape[0] // (4 * FRESH)):
            start = (j * 4 + part) * FRESH
            pieces.append(carry_ref[start : start + FRESH, :])
        for kv in kv_refs:
            start = 2 * SLOTS + part * FRESH
            pieces.append(kv[start : start + FRESH, :])
        return jnp.concatenate(pieces, axis=0)

    keys = fresh(0)
    keys = jnp.concatenate([keys, keys], axis=1)
    values = fresh(1).astype(F32).T
    ones = jnp.ones((VROWS - HD, values.shape[1]), F32)
    values_t = jnp.concatenate([values, ones], axis=0).astype(BF16)
    key_pos = fresh(2).astype(F32) * 128.0 + fresh(3).astype(F32)
    seen = jnp.concatenate([key_pos] * (HEAD_ROWS // TOK), axis=1) <= row_pos[...]

    def score(head):
        cols = slice(head * HEAD_ROWS, (head + 1) * HEAD_ROWS)
        s = jnp.dot(keys, rows_t[:, cols], preferred_element_type=F32)
        return jnp.where(seen, s, NEG)

    s = score(0)
    for head in range(HEADS):
        following = score(head + 1) if head + 1 < HEADS else None
        cols = slice(head * HEAD_ROWS, (head + 1) * HEAD_ROWS)
        update(s, values_t, cols, m_ref, acc_ref)
        s = following


def attend_body(first, last, sources, *refs):
    refs = list(refs)
    chunks = len(sources)
    len_ref = refs.pop(0)
    if first:
        q_refs = [refs.pop(0) for _ in range(4)]
    else:
        rows_t, row_pos, m_in, acc_in, carry_in = [refs.pop(0) for _ in range(5)]
    kv_refs = [refs.pop(0) for _ in range(chunks)]
    if last:
        out_refs = [refs.pop(0) for _ in range(4)]
    else:
        if first:
            rows_t, row_pos = refs.pop(0), refs.pop(0)
        m_out, acc_out, carry_out = [refs.pop(0) for _ in range(3)]
    if last:
        m_ref, acc_ref = refs.pop(0), refs.pop(0)
    else:
        m_ref, acc_ref = m_out, acc_out
    keys2, values_t, base_ref, s_ref = refs

    if first:
        for i, q_ref in enumerate(q_refs):
            for head in range(HEADS):
                q = q_ref[0:TOK, head * HD : (head + 1) * HD].astype(F32).T * TO_LOG2
                high = q.astype(BF16)
                cols = slice(head * HEAD_ROWS + i * TOK, head * HEAD_ROWS + (i + 1) * TOK)
                rows_t[0:HD, cols] = high
                rows_t[HD : 2 * HD, cols] = (q - high.astype(F32)).astype(BF16)
            coded = q_ref[TOK : TOK + 16, 0:TOK].astype(F32)
            row_pos[:, i * TOK : (i + 1) * TOK] = coded[0:1] * 128.0 + coded[1:2]
        m_ref[...] = jnp.full(m_ref.shape, NEG, F32)
        acc_ref[...] = jnp.zeros(acc_ref.shape, F32)
    else:
        m_ref[...] = m_in[...]
        acc_ref[...] = acc_in[...]

    x = lax.axis_index("xh") * 2 + lax.axis_index("xl")
    block_count = jnp.int32(0)
    for j, (step, swapped) in enumerate(sources):
        there = lax.rem(x + step, 4)
        group = y_index() * 2 + there // 2
        quarter = lax.rem(there, 2) * 2 + lax.rem(lax.axis_index("core") + swapped, 2)
        live = jnp.clip(len_ref[group] - quarter * SLOTS, 0, SLOTS)
        at = slice(j * SLOTS, (j + 1) * SLOTS)
        alive = lax.broadcasted_iota(jnp.int32, (SLOTS, HD), 0) < live
        k = kv_refs[j][0:SLOTS, :].astype(F32)
        k = jnp.where(alive, k, k[0:1, :]).astype(BF16)
        keys2[at, 0:HD] = k
        keys2[at, HD : 2 * HD] = k
        alive = lax.broadcasted_iota(jnp.int32, (VROWS, SLOTS), 1) < live
        v = jnp.concatenate(
            [kv_refs[j][SLOTS : 2 * SLOTS, :].astype(F32).T, jnp.ones((VROWS - HD, SLOTS), F32)],
            axis=0,
        )
        values_t[:, at] = jnp.where(alive, v, 0.0).astype(BF16)
        for b in range(SLOTS // BLOCK):
            base_ref[block_count] = j * SLOTS + b * BLOCK
            block_count += (live > b * BLOCK).astype(jnp.int32)

    if not last:
        held = 0 if first else carry_in.shape[0]
        if held:
            carry_out[0:held, :] = carry_in[...]
        for j, kv in enumerate(kv_refs):
            at = held + j * 4 * FRESH
            carry_out[at : at + 4 * FRESH, :] = kv[2 * SLOTS : 2 * SLOTS + 4 * FRESH, :]
    else:
        absorb_fresh(carry_in, kv_refs, rows_t, row_pos, m_ref, acc_ref)

    flash(block_count, base_ref, keys2, values_t, rows_t, m_ref, acc_ref, s_ref)

    if last:
        for i, out_ref in enumerate(out_refs):
            levels = []
            for head in range(HEADS):
                start = head * HEAD_ROWS + i * TOK
                cols = slice(start, start + TOK)
                total = acc_ref[HD : HD + 1, cols]
                out_ref[head * HD : (head + 1) * HD, :] = (acc_ref[0:HD, cols] / total).astype(BF16)
                levels.append(m_ref[:, cols] + jnp.log2(total))
            level = jnp.concatenate(levels, axis=0)
            high = level.astype(BF16).astype(F32)
            middle = (level - high).astype(BF16).astype(F32)
            low = level - high - middle
            stats = jnp.concatenate([high, middle, low, jnp.zeros((4, TOK), F32)], axis=0)
            out_ref[HEADS * HD : HEADS * HD + 16, :] = stats.astype(BF16)


def attend(first, last, lengths, state, sources, bundles):
    operands = [lengths, *state, *bundles]
    running = [jax.ShapeDtypeStruct((1, ROWS), F32), jax.ShapeDtypeStruct((VROWS, ROWS), F32)]
    scratch = []
    if last:
        outs = [jax.ShapeDtypeStruct((HEADS * HD + 16, TOK), BF16)] * 4
        scratch = [pltpu.VMEM(r.shape, r.dtype) for r in running]
    elif first:
        outs = [
            jax.ShapeDtypeStruct((2 * HD, ROWS), BF16),
            jax.ShapeDtypeStruct((1, HEAD_ROWS), F32),
        ] + running
    else:
        outs = running
    if not last:
        held = 0 if first else state[-1].shape[0]
        outs = outs + [jax.ShapeDtypeStruct((held + len(sources) * 4 * FRESH, HD), BF16)]
    slots = len(sources) * SLOTS
    scratch += [
        pltpu.VMEM((slots, 2 * HD), BF16),
        pltpu.VMEM((VROWS, slots), BF16),
        pltpu.SMEM((slots // BLOCK + 1,), jnp.int32),
        pltpu.VMEM((2, BLOCK, HEAD_ROWS), F32),
    ]
    return pl.pallas_call(
        lambda *refs: attend_body(first, last, sources, *refs),
        out_shape=outs,
        in_specs=[SMEM] + [VMEM] * (len(operands) - 1),
        out_specs=[VMEM] * len(outs),
        scratch_shapes=scratch,
        compiler_params=params(26),
        cost_estimate=pl.CostEstimate(
            flops=10**6, bytes_accessed=2**10, transcendentals=0
        ),
        name="attend",
    )(*operands)


def merge_body(*refs):
    parts, out_ref = refs[:-1], refs[-1]
    levels = []
    for part in parts:
        coded = part[HEADS * HD : HEADS * HD + 16, :].astype(F32)
        levels.append(coded[0:4] + coded[4:8] + coded[8:12])
    top = levels[0]
    for level in levels[1:]:
        top = jnp.maximum(top, level)
    weights = [jnp.exp2(level - top) for level in levels]
    total = weights[0] + weights[1] + weights[2] + weights[3]
    weights = [w / total for w in weights]
    for head in range(HEADS):
        mixed = None
        for part, w in zip(parts, weights):
            term = part[head * HD : (head + 1) * HD, :].astype(F32) * w[head : head + 1]
            mixed = term if mixed is None else mixed + term
        out_ref[:, head * HD : (head + 1) * HD] = mixed.T.astype(BF16)


def merge(parts):
    return pl.pallas_call(
        merge_body,
        out_shape=jax.ShapeDtypeStruct((TOK, HEADS * HD), BF16),
        in_specs=[VMEM] * 4,
        out_specs=VMEM,
        compiler_params=params(4),
        name="merge",
    )(*parts)


def project_body(*refs):
    x_own, x_other = refs[0:2]
    weights = refs[2:6]
    outs = refs[6:24]
    x_ref, w_ref, sems = refs[24:27]
    depth = weights[0].shape[0]
    copies = [
        pltpu.make_async_copy(
            weight, w_ref.at[i // 2, pl.ds((i % 2) * depth, depth)], sems.at[i]
        )
        for i, weight in enumerate(weights)
    ]
    for copy in copies:
        copy.start()
    z = lax.axis_index("z")
    for r in range(8):
        part = pl.multiple_of(lax.rem(z + r, 8) * 16, 16)
        for j in range(4):
            row = r * 64 + j * 16
            source = pl.ds(pl.multiple_of(part + j * TOK, 16), 16)
            x_ref[row : row + 16, 0:depth] = x_own[source, :]
            x_ref[row : row + 16, depth : 2 * depth] = x_other[source, :]
    for copy in copies:
        copy.wait()
    for side in range(2):
        out = outs[side * 9 : side * 9 + 9]
        for n in range(4):
            cols = slice(n * 256, (n + 1) * 256)
            y = jnp.dot(x_ref[...], w_ref[side, :, cols], preferred_element_type=F32).astype(BF16)
            for r in range(8):
                if r < 4:
                    out[r][:, cols] = y[r * 64 : (r + 1) * 64]
                elif r == 4:
                    out[4][:, cols] = y[256:288]
                    out[5][:, cols] = y[288:320]
                else:
                    out[r + 1][:, cols] = y[r * 64 : (r + 1) * 64]


def project(x_own, x_other, weights):
    full = jax.ShapeDtypeStruct((64, WIDE), BF16)
    half = jax.ShapeDtypeStruct((32, WIDE), BF16)
    outs = pl.pallas_call(
        project_body,
        out_shape=([full] * 4 + [half] * 2 + [full] * 3) * 2,
        in_specs=[VMEM] * 2 + [HBM] * 4,
        out_specs=[VMEM] * 18,
        scratch_shapes=[
            pltpu.VMEM((512, 1024), BF16),
            pltpu.VMEM((2, 1024, WIDE), BF16),
            pltpu.SemaphoreType.DMA((4,)),
        ],
        compiler_params=params(16),
        name="project",
    )(x_own, x_other, *weights)
    return outs[:9], outs[9:]


def sum_bf16(a, b):
    return (a.astype(F32) + b.astype(F32)).astype(BF16)


def sum_over_z(parts):
    up = along_z(parts[4], 1)
    down = along_z(parts[5], -1)
    p3 = parts[3]
    half = p3.shape[0] // 2
    up = jnp.concatenate([sum_bf16(p3[:half], up), p3[half:]], axis=0)
    p5 = parts[6]
    down = jnp.concatenate([p5[:half], sum_bf16(p5[half:], down)], axis=0)
    for r in (2, 1):
        up = sum_bf16(parts[r], along_z(up, 1))
        down = sum_bf16(parts[9 - r], along_z(down, -1))
    return parts[0], along_z(up, 1), along_z(down, -1)


def order_body(*refs):
    out_ref = refs[6]
    yp, yl, xh = (lax.axis_index(name) for name in ("yp", "yl", "xh"))
    for side in range(2):
        kept, up, down = refs[side * 3 : side * 3 + 3]
        total = kept[...].astype(F32) + up[...].astype(F32) + down[...].astype(F32)
        total = total.astype(BF16)
        column = pl.ds(pl.multiple_of((yl if side == 0 else 1 - yl) * WIDE, WIDE), WIDE)
        for j in range(4):
            place = (yp if j % 2 == 0 else 1 - yp) * 2 + (xh if j < 2 else 1 - xh)
            out_ref[place, :, column] = total[j * 16 : (j + 1) * 16]


def ordered(sums):
    return pl.pallas_call(
        order_body,
        out_shape=jax.ShapeDtypeStruct((4, 16, 2 * WIDE), BF16),
        in_specs=[VMEM] * 6,
        out_specs=VMEM,
        compiler_params=params(4),
        name="ordered",
    )(*sums)


def finish_body(spread_ref, out_ref, sum_ref):
    yl = lax.axis_index("yl")
    for side in range(2):
        cols = slice(side * WIDE, (side + 1) * WIDE)
        for p in range(2):
            for xh in range(2):
                for core in range(2):
                    first = (p * 2 + xh) * 16 + core * 4
                    sum_ref[p, xh, core] = (
                        spread_ref[first : first + 4, cols].astype(F32)
                        + spread_ref[first + 8 : first + 12, cols].astype(F32)
                    )
        own = yl == side
        for p in range(2):
            for xh in range(2):
                for core in range(2):
                    value = sum_ref[p, xh, core]
                    if core == 1:
                        value = jnp.where(own, value, sum_ref[1 - p, xh, core])
                    start = (((p * 2 + side) * 2 + xh) * 2 + core) * WIDE
                    out_ref[:, start : start + WIDE] = value.astype(BF16)


def finish(spread):
    return pl.pallas_call(
        finish_body,
        out_shape=jax.ShapeDtypeStruct((4, 16 * WIDE), BF16),
        in_specs=[VMEM],
        out_specs=VMEM,
        scratch_shapes=[pltpu.VMEM((2, 2, 2, 4, WIDE), F32)],
        compiler_params=params(4),
        name="finish",
    )(spread)


def shards(
    queries, cache_keys, cache_values, new_keys, new_values, out_weight, cache_lengths, positions
):
    q_ext, kv = pack(
        queries, cache_keys[0, 0], cache_values[0, 0], new_keys, new_values, positions[None, :]
    )
    left, right = along_x(kv, 1), along_x(kv, -1)
    q_prev, q_next, q_far = along_y(q_ext, 1), along_y(q_ext, -1), along_y(q_ext, 2)
    q_all = (q_prev, q_next, q_far)
    w_kept, w_away = halves(after(out_weight, q_prev))
    other = to_other_core(after(kv, q_all))
    w_kept_pair, w_away_pair = to_y_pair(w_kept, 0), to_y_pair(w_away, 1)
    left, right = after((left, right), w_kept)
    far = along_x(after(kv, (left, right)), 2)
    rows_t, row_pos, m, acc, carry = attend(
        True,
        False,
        cache_lengths,
        (q_ext, *q_all),
        ((0, 0), (0, 1), (3, 0), (1, 0)),
        (kv, other, left, right),
    )
    left_other, right_other = to_other_core(left), to_other_core(right)
    far_other = to_other_core(after(far, m))
    mine, prev, following, distant = attend(
        False,
        True,
        cache_lengths,
        (rows_t, row_pos, m, acc, carry),
        ((3, 1), (1, 1), (2, 0), (2, 1)),
        (left_other, right_other, far, far_other),
    )
    attended = merge((mine, along_y(prev, -1), along_y(following, 1), along_y(distant, 2)))

    attended, w_kept_pair, w_away_pair = lax.optimization_barrier(
        (attended, w_kept_pair, w_away_pair)
    )
    w_other, w_other_pair = to_other_core(w_away), to_other_core(w_away_pair)

    corner = lax.ppermute(attended, ("yp", "xh"), [(i, 3 - i) for i in range(4)])
    blocks = (attended, along_y(attended, 2), along_x(attended, 2), corner)
    x_own = jnp.concatenate(blocks, axis=0)
    weights = (w_kept, w_other, w_kept_pair, w_other_pair)
    near, pair = project(x_own, to_other_core(x_own), weights)
    blocks = ordered((*sum_over_z(near), *sum_over_z(pair))).reshape(64, 2 * WIDE)
    spread = lax.all_to_all(blocks, ("yp", "xh", "xl", "core"), 0, 0, tiled=True)
    return finish(spread)


def solution(mesh):
    fine = Mesh(
        mesh.devices.reshape(2, 2, 2, 8, 2, 2), ("yp", "yl", "xh", "z", "xl", "core")
    )
    seq, head = ("yp", "yl", "xh"), ("z", "xl", "core")
    placed = (
        P(seq, head),
        P(seq, head, None, None),
        P(seq, head, None, None),
        P(seq, None),
        P(seq, None),
        P(head, seq),
        P(),
        P(seq),
    )
    return jax.shard_map(
        shards, mesh=fine, in_specs=placed, out_specs=P(seq + head, None), check_vma=False
    )
```

profile of v0, /device:TPU:1, one launch (start us, length us, event | category | flops | bytes accessed | tf_op | source)
XLA Modules:
  0.0 129.6 jit_solution(7107742409444323572)
XLA Ops:
  0.0 2.7 %pack.1 = (bf16[144,512]{1,0:T(8,128)(2,1)}, bf16[2176,128]{1,0:T(8,128)(2,1)}) custom-call(bf16[128,512]{1,0:T(8,128)(2,1)} %q_hbm.1, bf16[1024,128]{1,0:T(8,128)(2,1)} %bitcast.3, bf16[1024,128]{1,0:T(8,128)(2,1)} %bitcast.4, bf16[128,1024]{1,0:T(8,128)(2,1)} %nk_hbm.1, bf16[128,1024]{1,0:T(8,128)(2,1)} %nv_hbm.1, s32[1,128]{1,0:T(1,128)} %bitcast.5), custom_call_target="tpu_custom_call" | custom-call | tf_op jit(solution)/shard_map/pack/pallas_call | solution.py:106
  2.7 2.1 %collective-permute-start.4 = (bf16[2176,128]{1,0:T(8,128)(2,1)}, bf16[2176,128]{1,0:T(8,128)(2,1)S(1)}, u32[]{:S(2)}, u32[]{:S(2)}) collective-permute-start(bf16[2176,128]{1,0:T(8,128)(2,1)} %get-tuple-element.57.refs_5_), channel_id=1, source_target_pairs={{0,2},{2,32},{32,34},{34,0},{1,3},{3,33},{33,35},{35,1},{4,6},{6,3... | collective-permute-start | bytes 1671176 | tf_op jit(solution)/shard_map/ppermute | solution.py:30
  4.8 1.4 %collective-permute-start.5 = (bf16[2176,128]{1,0:T(8,128)(2,1)}, bf16[2176,128]{1,0:T(8,128)(2,1)S(1)}, u32[]{:S(2)}, u32[]{:S(2)}) collective-permute-start(bf16[2176,128]{1,0:T(8,128)(2,1)} %get-tuple-element.57.refs_5_), channel_id=1, source_target_pairs={{0,34},{2,0},{32,2},{34,32},{1,35},{3,1},{33,3},{35,33},{4,38},{6,... | collective-permute-start | bytes 1671176 | tf_op jit(solution)/shard_map/ppermute | solution.py:30
  6.2 1.4 %collective-permute-start = (bf16[144,512]{1,0:T(8,128)(2,1)}, bf16[144,512]{1,0:T(8,128)(2,1)S(1)}, u32[]{:S(2)}, u32[]{:S(2)}) collective-permute-start(bf16[144,512]{1,0:T(8,128)(2,1)} %get-tuple-element.45.refs_1_), channel_id=1, source_target_pairs={{0,64},{64,128},{128,192},{192,0},{1,65},{65,129},{129,193},{193,1... | collective-permute-start | bytes 442376 | tf_op jit(solution)/shard_map/ppermute | solution.py:30
  7.6 1.4 %collective-permute-start.1 = (bf16[144,512]{1,0:T(8,128)(2,1)}, bf16[144,512]{1,0:T(8,128)(2,1)S(1)}, u32[]{:S(2)}, u32[]{:S(2)}) collective-permute-start(bf16[144,512]{1,0:T(8,128)(2,1)} %get-tuple-element.45.refs_1_), channel_id=1, source_target_pairs={{0,192},{64,0},{128,64},{192,128},{1,193},{65,1},{129,65},{193,129... | collective-permute-start | bytes 442376 | tf_op jit(solution)/shard_map/ppermute | solution.py:30
  9.0 1.6 %collective-permute-start.2 = (bf16[144,512]{1,0:T(8,128)(2,1)}, bf16[144,512]{1,0:T(8,128)(2,1)S(1)}, u32[]{:S(2)}, u32[]{:S(2)}) collective-permute-start(bf16[144,512]{1,0:T(8,128)(2,1)} %get-tuple-element.45.refs_1_), channel_id=1, source_target_pairs={{0,128},{64,192},{128,0},{192,64},{1,129},{65,193},{129,1},{193,65... | collective-permute-start | bytes 442376 | tf_op jit(solution)/shard_map/ppermute | solution.py:30
  10.7 1.4 %collective-permute-done.refs_2_ = bf16[144,512]{1,0:T(8,128)(2,1)S(1)} collective-permute-done((bf16[144,512]{1,0:T(8,128)(2,1)}, bf16[144,512]{1,0:T(8,128)(2,1)S(1)}, u32[]{:S(2)}, u32[]{:S(2)}) %collective-permute-start) | collective-permute-done | bytes 147488 | tf_op jit(solution)/shard_map/ppermute | solution.py:30
  12.1 2.9 %halves.1 = (bf16[512,1024]{1,0:T(8,128)(2,1)}, bf16[512,1024]{1,0:T(8,128)(2,1)}) custom-call(bf16[512,2048]{1,0:T(8,128)(2,1)} %w_hbm), custom_call_target="tpu_custom_call" | custom-call | tf_op jit(solution)/shard_map/halves/pallas_call | solution.py:134
  16.3 3.9 %collective-permute-start.3 = (bf16[2176,128]{1,0:T(8,128)(2,1)S(1)}, bf16[2176,128]{1,0:T(8,128)(2,1)S(1)}, u32[]{:S(2)}, u32[]{:S(2)}) collective-permute-start(bf16[2176,128]{1,0:T(8,128)(2,1)S(1)} %copy-done.1), channel_id=1, source_target_pairs={{0,1},{1,0},{2,3},{3,2},{4,5},{5,4},{6,7},{7,6},{8,9},{9,8},{10,11... | collective-permute-start | bytes 1671176 | tf_op jit(solution)/shard_map/ppermute | solution.py:30
  20.4 3.0 %collective-permute-start.13 = (bf16[512,1024]{1,0:T(8,128)(2,1)}, bf16[512,1024]{1,0:T(8,128)(2,1)S(1)}, u32[]{:S(2)}, u32[]{:S(2)}) collective-permute-start(bf16[512,1024]{1,0:T(8,128)(2,1)} %get-tuple-element.49.refs_2_), channel_id=1, source_target_pairs={{0,64},{1,193},{64,0},{65,129},{128,192},{129,65},{192,128},{193,1... | collective-permute-start | bytes 3145736 | tf_op jit(solution)/shard_map/ppermute | solution.py:43
  23.4 3.2 %collective-permute-start.6 = (bf16[2176,128]{1,0:T(8,128)(2,1)S(1)}, bf16[2176,128]{1,0:T(8,128)(2,1)S(1)}, u32[]{:S(2)}, u32[]{:S(2)}) collective-permute-start(bf16[2176,128]{1,0:T(8,128)(2,1)S(1)} %collective-permute-done.4.refs_7_), channel_id=1, source_target_pairs={{0,1},{1,0},{2,3},{3,2},{4,5},{5,4},{6,7},{7,6},{8,9},{9,8},{10,11... | collective-permute-start | bytes 1671176 | tf_op jit(solution)/shard_map/ppermute | solution.py:30
  26.6 7.0 %attend.2 = (bf16[256,2048]{1,0:T(8,128)(2,1)S(1)}, f32[1,512]{1,0:T(1,128)S(1)}, f32[1,2048]{1,0:T(1,128)S(1)}, f32[144,2048]{1,0:T(8,128)S(1)}, bf16[512,128]{1,0:T(8,128)(2,1)S(1)}) custom-call(s32[8]{0:T(128)S(1)} %copy-done.3, bf16[144,512]{1,0:T(8,128)(2,1)S(1)} %copy-done.2, bf16[144,512]{1,0:T(8,128)(2,1)S(1)} %collective-permute-done.refs_2_, ...), custom_call_target="tpu_custom_call" | custom-call | flops 1000000 | bytes 1024 | tf_op jit(solution)/shard_map/attend/pallas_call | solution.py:327
  33.6 2.4 %collective-permute-done.8.refs_8_ = bf16[2176,128]{1,0:T(8,128)(2,1)S(1)} collective-permute-done((bf16[2176,128]{1,0:T(8,128)(2,1)S(1)}, bf16[2176,128]{1,0:T(8,128)(2,1)S(1)}, u32[]{:S(2)}, u32[]{:S(2)}) %collective-permute-start.8) | collective-permute-done | bytes 557088 | tf_op jit(solution)/shard_map/ppermute | solution.py:30
  36.8 1.6 %collective-permute-done.9.refs_9_ = bf16[2176,128]{1,0:T(8,128)(2,1)S(1)} collective-permute-done((bf16[2176,128]{1,0:T(8,128)(2,1)S(1)}, bf16[2176,128]{1,0:T(8,128)(2,1)S(1)}, u32[]{:S(2)}, u32[]{:S(2)}) %collective-permute-start.9) | collective-permute-done | bytes 557088 | tf_op jit(solution)/shard_map/ppermute | solution.py:30
  38.4 10.5 %attend.3 = (bf16[528,128]{1,0:T(8,128)(2,1)S(1)}, bf16[528,128]{1,0:T(8,128)(2,1)S(1)}, bf16[528,128]{1,0:T(8,128)(2,1)S(1)}, bf16[528,128]{1,0:T(8,128)(2,1)S(1)}) custom-call(s32[8]{0:T(128)S(1)} %copy-done.3, bf16[256,2048]{1,0:T(8,128)(2,1)S(1)} %get-tuple-element.52.refs_1_, f32[1,512]{1,0:T(1,128)S(1)} %get-tuple-element.53.refs_2_, ...), custom_call_target="tpu_custom_call" | custom-call | flops 1000000 | bytes 1024 | tf_op jit(solution)/shard_map/attend/pallas_call | solution.py:327
  53.8 5.0 %collective-permute-done.11.refs_2_ = bf16[528,128]{1,0:T(8,128)(2,1)S(1)} collective-permute-done((bf16[528,128]{1,0:T(8,128)(2,1)S(1)}, bf16[528,128]{1,0:T(8,128)(2,1)S(1)}, u32[]{:S(2)}, u32[]{:S(2)}) %collective-permute-start.11) | collective-permute-done | bytes 135200 | tf_op jit(solution)/shard_map/ppermute | solution.py:30
  59.0 1.4 %collective-permute-start.20 = (bf16[512,1024]{1,0:T(8,128)(2,1)S(1)}, bf16[512,1024]{1,0:T(8,128)(2,1)S(1)}, u32[]{:S(2)}, u32[]{:S(2)}) collective-permute-start(bf16[512,1024]{1,0:T(8,128)(2,1)S(1)} %collective-permute-done.14), channel_id=1, source_target_pairs={{0,1},{1,0},{2,3},{3,2},{4,5},{5,4},{6,7},{7,6},{8,9},{9,8},{10,11... | collective-permute-start | bytes 3145736 | tf_op jit(solution)/shard_map/ppermute | solution.py:30
  61.2 5.0 %collective-permute-start.17 = (bf16[128,512]{1,0:T(8,128)(2,1)S(1)}, bf16[128,512]{1,0:T(8,128)(2,1)S(1)}, u32[]{:S(2)}, u32[]{:S(2)}) collective-permute-start(bf16[128,512]{1,0:T(8,128)(2,1)S(1)} %merge.1), channel_id=1, source_target_pairs={{0,160},{32,128},{128,32},{160,0},{1,161},{33,129},{129,33},{161,1... | collective-permute-start | bytes 393224 | tf_op jit(solution)/shard_map/ppermute | solution.py:546
  67.5 4.7 %collective-permute-done.17 = bf16[128,512]{1,0:T(8,128)(2,1)S(1)} collective-permute-done((bf16[128,512]{1,0:T(8,128)(2,1)S(1)}, bf16[128,512]{1,0:T(8,128)(2,1)S(1)}, u32[]{:S(2)}, u32[]{:S(2)}) %collective-permute-start.17) | collective-permute-done | bytes 131104 | tf_op jit(solution)/shard_map/ppermute | solution.py:546
  73.5 1.5 %collective-permute-done.18.refs_1_ = bf16[512,512]{1,0:T(8,128)(2,1)S(1)} collective-permute-done((bf16[512,512]{1,0:T(8,128)(2,1)S(1)}, bf16[512,512]{1,0:T(8,128)(2,1)S(1)}, u32[]{:S(2)}, u32[]{:S(2)}) %collective-permute-start.18) | collective-permute-done | bytes 524320 | tf_op jit(solution)/shard_map/ppermute | solution.py:30
  75.0 2.7 %project.1 = (bf16[64,1024]{1,0:T(8,128)(2,1)S(1)}, bf16[64,1024]{1,0:T(8,128)(2,1)S(1)}, bf16[64,1024]{1,0:T(8,128)(2,1)S(1)}, bf16[64,1024]{1,0:T(8,128)(2,1)S...) custom-call(bf16[512,512]{1,0:T(8,128)(2,1)S(1)} %constant_dynamic-u, ...), custom_call_target="tpu_custom_call" | custom-call | tf_op jit(solution)/shard_map/project/pallas_call | solution.py:414
  77.7 5.6 %collective-permute-start.33 = (bf16[32,1024]{1,0:T(8,128)(2,1)S(1)}, bf16[32,1024]{1,0:T(8,128)(2,1)S(1)}, u32[]{:S(2)}, u32[]{:S(2)}) collective-permute-start(bf16[32,1024]{1,0:T(8,128)(2,1)S(1)} %get-tuple-element.84), channel_id=1, source_target_pairs={{0,28},{4,0},{8,4},{12,8},{16,12},{20,16},{24,20},{28,24},{1,29},{... | collective-permute-start | bytes 196616 | tf_op jit(solution)/shard_map/ppermute | solution.py:30
  83.4 2.7 %collective-permute-start.25 = (bf16[32,1024]{1,0:T(8,128)(2,1)S(1)}, bf16[32,1024]{1,0:T(8,128)(2,1)S(1)}, u32[]{:S(2)}, u32[]{:S(2)}) collective-permute-start(bf16[32,1024]{1,0:T(8,128)(2,1)S(1)} %get-tuple-element.75), channel_id=1, source_target_pairs={{0,28},{4,0},{8,4},{12,8},{16,12},{20,16},{24,20},{28,24},{1,29},{... | collective-permute-start | bytes 196616 | tf_op jit(solution)/shard_map/ppermute | solution.py:30
  86.2 2.7 %collective-permute-start.34 = (bf16[64,1024]{1,0:T(8,128)(2,1)S(1)}, bf16[64,1024]{1,0:T(8,128)(2,1)S(1)}, u32[]{:S(2)}, u32[]{:S(2)}) collective-permute-start(bf16[64,1024]{1,0:T(8,128)(2,1)S(1)} %pad_maximum_fusion.3), channel_id=1, source_target_pairs={{0,28},{4,0},{8,4},{12,8},{16,12},{20,16},{24,20},{28,24},{1,29},{... | collective-permute-start | bytes 393224 | tf_op jit(solution)/shard_map/ppermute | solution.py:30
  89.1 2.7 %collective-permute-start.26 = (bf16[64,1024]{1,0:T(8,128)(2,1)S(1)}, bf16[64,1024]{1,0:T(8,128)(2,1)S(1)}, u32[]{:S(2)}, u32[]{:S(2)}) collective-permute-start(bf16[64,1024]{1,0:T(8,128)(2,1)S(1)} %pad_maximum_fusion.1), channel_id=1, source_target_pairs={{0,28},{4,0},{8,4},{12,8},{16,12},{20,16},{24,20},{28,24},{1,29},{... | collective-permute-start | bytes 393224 | tf_op jit(solution)/shard_map/ppermute | solution.py:30
  92.0 2.7 %collective-permute-start.35 = (bf16[64,1024]{1,0:T(8,128)(2,1)S(1)}, bf16[64,1024]{1,0:T(8,128)(2,1)S(1)}, u32[]{:S(2)}, u32[]{:S(2)}) collective-permute-start(bf16[64,1024]{1,0:T(8,128)(2,1)S(1)} %add_convert_fusion.1), channel_id=1, source_target_pairs={{0,28},{4,0},{8,4},{12,8},{16,12},{20,16},{24,20},{28,24},{1,29},{... | collective-permute-start | bytes 393224 | tf_op jit(solution)/shard_map/ppermute | solution.py:30
  94.9 2.7 %collective-permute-start.27 = (bf16[64,1024]{1,0:T(8,128)(2,1)S(1)}, bf16[64,1024]{1,0:T(8,128)(2,1)S(1)}, u32[]{:S(2)}, u32[]{:S(2)}) collective-permute-start(bf16[64,1024]{1,0:T(8,128)(2,1)S(1)} %add_convert_fusion.5), channel_id=1, source_target_pairs={{0,28},{4,0},{8,4},{12,8},{16,12},{20,16},{24,20},{28,24},{1,29},{... | collective-permute-start | bytes 393224 | tf_op jit(solution)/shard_map/ppermute | solution.py:30
  97.9 3.0 %collective-permute-start.36 = (bf16[64,1024]{1,0:T(8,128)(2,1)S(1)}, bf16[64,1024]{1,0:T(8,128)(2,1)S(1)}, u32[]{:S(2)}, u32[]{:S(2)}) collective-permute-start(bf16[64,1024]{1,0:T(8,128)(2,1)S(1)} %add_convert_fusion), channel_id=1, source_target_pairs={{0,28},{4,0},{8,4},{12,8},{16,12},{20,16},{24,20},{28,24},{1,29},{... | collective-permute-start | bytes 393224 | tf_op jit(solution)/shard_map/ppermute | solution.py:30
  101.5 2.8 %collective-permute-start.28 = (bf16[64,1024]{1,0:T(8,128)(2,1)S(1)}, bf16[64,1024]{1,0:T(8,128)(2,1)S(1)}, u32[]{:S(2)}, u32[]{:S(2)}) collective-permute-start(bf16[64,1024]{1,0:T(8,128)(2,1)S(1)} %add_convert_fusion.4), channel_id=1, source_target_pairs={{0,28},{4,0},{8,4},{12,8},{16,12},{20,16},{24,20},{28,24},{1,29},{... | collective-permute-start | bytes 393224 | tf_op jit(solution)/shard_map/ppermute | solution.py:30
  104.5 2.9 %collective-permute-done.32.refs_4_ = bf16[64,1024]{1,0:T(8,128)(2,1)S(1)} collective-permute-done((bf16[64,1024]{1,0:T(8,128)(2,1)S(1)}, bf16[64,1024]{1,0:T(8,128)(2,1)S(1)}, u32[]{:S(2)}, u32[]{:S(2)}) %collective-permute-start.32) | collective-permute-done | bytes 131104 | tf_op jit(solution)/shard_map/ppermute | solution.py:30
  107.4 2.5 %collective-permute-done.24.refs_1_ = bf16[64,1024]{1,0:T(8,128)(2,1)S(1)} collective-permute-done((bf16[64,1024]{1,0:T(8,128)(2,1)S(1)}, bf16[64,1024]{1,0:T(8,128)(2,1)S(1)}, u32[]{:S(2)}, u32[]{:S(2)}) %collective-permute-start.24) | collective-permute-done | bytes 131104 | tf_op jit(solution)/shard_map/ppermute | solution.py:30
  110.0 18.7 %all_to_all.11 = bf16[16,4,2048]{2,1,0:T(4,128)(2,1)S(1)} all-to-all(bf16[16,4,2048]{2,1,0:T(4,128)(2,1)S(1)} %all_to_all.7), channel_id=1, replica_groups=mesh['yp'=2,'yl'=2,'xh'=2,'z'=8,'xl'=2,'core'=2] {'yp','xh','xl','core'}, dimensions={0} | all-to-all | bytes 524288 | tf_op jit(solution)/shard_map/all_to_all | solution.py:552
  (87 shorter events, 13.3 us)
Async XLA Ops:
  2.7 17.5 %collective-permute-start.4 = (bf16[2176,128]{1,0:T(8,128)(2,1)}, bf16[2176,128]{1,0:T(8,128)(2,1)S(1)}, u32[]{:S(2)}, u32[]{:S(2)}) collective-permute-start(bf16[2176,128]{1,0:T(8,128)(2,1)} %get-tuple-element.57.refs_5_), channel_id=1, source_target_pairs={{0,2},{2,32},{32,34},{34,0},{1,3},{3,33},{33,35},{35,1},{4,6},{6,3... | collective-permute-start | bytes 1671176 | tf_op jit(solution)/shard_map/ppermute | solution.py:30
  4.8 15.4 %collective-permute-start.5 = (bf16[2176,128]{1,0:T(8,128)(2,1)}, bf16[2176,128]{1,0:T(8,128)(2,1)S(1)}, u32[]{:S(2)}, u32[]{:S(2)}) collective-permute-start(bf16[2176,128]{1,0:T(8,128)(2,1)} %get-tuple-element.57.refs_5_), channel_id=1, source_target_pairs={{0,34},{2,0},{32,2},{34,32},{1,35},{3,1},{33,3},{35,33},{4,38},{6,... | collective-permute-start | bytes 1671176 | tf_op jit(solution)/shard_map/ppermute | solution.py:30
  6.2 5.9 %collective-permute-start = (bf16[144,512]{1,0:T(8,128)(2,1)}, bf16[144,512]{1,0:T(8,128)(2,1)S(1)}, u32[]{:S(2)}, u32[]{:S(2)}) collective-permute-start(bf16[144,512]{1,0:T(8,128)(2,1)} %get-tuple-element.45.refs_1_), channel_id=1, source_target_pairs={{0,64},{64,128},{128,192},{192,0},{1,65},{65,129},{129,193},{193,1... | collective-permute-start | bytes 442376 | tf_op jit(solution)/shard_map/ppermute | solution.py:30
  7.6 7.4 %collective-permute-start.1 = (bf16[144,512]{1,0:T(8,128)(2,1)}, bf16[144,512]{1,0:T(8,128)(2,1)S(1)}, u32[]{:S(2)}, u32[]{:S(2)}) collective-permute-start(bf16[144,512]{1,0:T(8,128)(2,1)} %get-tuple-element.45.refs_1_), channel_id=1, source_target_pairs={{0,192},{64,0},{128,64},{192,128},{1,193},{65,1},{129,65},{193,129... | collective-permute-start | bytes 442376 | tf_op jit(solution)/shard_map/ppermute | solution.py:30
  9.0 7.3 %collective-permute-start.2 = (bf16[144,512]{1,0:T(8,128)(2,1)}, bf16[144,512]{1,0:T(8,128)(2,1)S(1)}, u32[]{:S(2)}, u32[]{:S(2)}) collective-permute-start(bf16[144,512]{1,0:T(8,128)(2,1)} %get-tuple-element.45.refs_1_), channel_id=1, source_target_pairs={{0,128},{64,192},{128,0},{192,64},{1,129},{65,193},{129,1},{193,65... | collective-permute-start | bytes 442376 | tf_op jit(solution)/shard_map/ppermute | solution.py:30
  16.3 10.2 %collective-permute-start.3 = (bf16[2176,128]{1,0:T(8,128)(2,1)S(1)}, bf16[2176,128]{1,0:T(8,128)(2,1)S(1)}, u32[]{:S(2)}, u32[]{:S(2)}) collective-permute-start(bf16[2176,128]{1,0:T(8,128)(2,1)S(1)} %copy-done.1), channel_id=1, source_target_pairs={{0,1},{1,0},{2,3},{3,2},{4,5},{5,4},{6,7},{7,6},{8,9},{9,8},{10,11... | collective-permute-start | bytes 1671176 | tf_op jit(solution)/shard_map/ppermute | solution.py:30
  20.2 15.7 %collective-permute-start.8 = (bf16[2176,128]{1,0:T(8,128)(2,1)S(1)}, bf16[2176,128]{1,0:T(8,128)(2,1)S(1)}, u32[]{:S(2)}, u32[]{:S(2)}) collective-permute-start(bf16[2176,128]{1,0:T(8,128)(2,1)S(1)} %copy-done.1), channel_id=1, source_target_pairs={{0,32},{2,34},{32,0},{34,2},{1,33},{3,35},{33,1},{35,3},{4,36},{6,... | collective-permute-start | bytes 1671176 | tf_op jit(solution)/shard_map/ppermute | solution.py:30
  20.4 38.6 %collective-permute-start.13 = (bf16[512,1024]{1,0:T(8,128)(2,1)}, bf16[512,1024]{1,0:T(8,128)(2,1)S(1)}, u32[]{:S(2)}, u32[]{:S(2)}) collective-permute-start(bf16[512,1024]{1,0:T(8,128)(2,1)} %get-tuple-element.49.refs_2_), channel_id=1, source_target_pairs={{0,64},{1,193},{64,0},{65,129},{128,192},{129,65},{192,128},{193,1... | collective-permute-start | bytes 3145736 | tf_op jit(solution)/shard_map/ppermute | solution.py:43
  23.4 35.6 %collective-permute-start.14 = (bf16[512,1024]{1,0:T(8,128)(2,1)}, bf16[512,1024]{1,0:T(8,128)(2,1)S(1)}, u32[]{:S(2)}, u32[]{:S(2)}) collective-permute-start(bf16[512,1024]{1,0:T(8,128)(2,1)} %get-tuple-element.63), channel_id=1, source_target_pairs={{0,192},{1,65},{64,128},{65,1},{128,64},{129,193},{192,0},{193,129... | collective-permute-start | bytes 3145736 | tf_op jit(solution)/shard_map/ppermute | solution.py:43
  23.4 13.4 %collective-permute-start.6 = (bf16[2176,128]{1,0:T(8,128)(2,1)S(1)}, bf16[2176,128]{1,0:T(8,128)(2,1)S(1)}, u32[]{:S(2)}, u32[]{:S(2)}) collective-permute-start(bf16[2176,128]{1,0:T(8,128)(2,1)S(1)} %collective-permute-done.4.refs_7_), channel_id=1, source_target_pairs={{0,1},{1,0},{2,3},{3,2},{4,5},{5,4},{6,7},{7,6},{8,9},{9,8},{10,11... | collective-permute-start | bytes 1671176 | tf_op jit(solution)/shard_map/ppermute | solution.py:30
  26.6 10.3 %collective-permute-start.7 = (bf16[2176,128]{1,0:T(8,128)(2,1)S(1)}, bf16[2176,128]{1,0:T(8,128)(2,1)S(1)}, u32[]{:S(2)}, u32[]{:S(2)}) collective-permute-start(bf16[2176,128]{1,0:T(8,128)(2,1)S(1)} %collective-permute-done.5.refs_8_), channel_id=1, source_target_pairs={{0,1},{1,0},{2,3},{3,2},{4,5},{5,4},{6,7},{7,6},{8,9},{9,8},{10,11... | collective-permute-start | bytes 1671176 | tf_op jit(solution)/shard_map/ppermute | solution.py:30
  50.0 8.8 %collective-permute-start.11 = (bf16[528,128]{1,0:T(8,128)(2,1)S(1)}, bf16[528,128]{1,0:T(8,128)(2,1)S(1)}, u32[]{:S(2)}, u32[]{:S(2)}) collective-permute-start(bf16[528,128]{1,0:T(8,128)(2,1)S(1)} %get-tuple-element.61), channel_id=1, source_target_pairs={{0,64},{64,128},{128,192},{192,0},{1,65},{65,129},{129,193},{193,1... | collective-permute-start | bytes 405512 | tf_op jit(solution)/shard_map/ppermute | solution.py:30
  50.5 8.3 %collective-permute-start.12 = (bf16[528,128]{1,0:T(8,128)(2,1)S(1)}, bf16[528,128]{1,0:T(8,128)(2,1)S(1)}, u32[]{:S(2)}, u32[]{:S(2)}) collective-permute-start(bf16[528,128]{1,0:T(8,128)(2,1)S(1)} %get-tuple-element.62), channel_id=1, source_target_pairs={{0,128},{64,192},{128,0},{192,64},{1,129},{65,193},{129,1},{193,65... | collective-permute-start | bytes 405512 | tf_op jit(solution)/shard_map/ppermute | solution.py:30
  52.9 20.6 %collective-permute-start.19 = (bf16[512,1024]{1,0:T(8,128)(2,1)S(1)}, bf16[512,1024]{1,0:T(8,128)(2,1)S(1)}, u32[]{:S(2)}, u32[]{:S(2)}) collective-permute-start(bf16[512,1024]{1,0:T(8,128)(2,1)S(1)} %copy-done.4), channel_id=1, source_target_pairs={{0,1},{1,0},{2,3},{3,2},{4,5},{5,4},{6,7},{7,6},{8,9},{9,8},{10,11... | collective-permute-start | bytes 3145736 | tf_op jit(solution)/shard_map/ppermute | solution.py:30
  59.0 16.0 %collective-permute-start.20 = (bf16[512,1024]{1,0:T(8,128)(2,1)S(1)}, bf16[512,1024]{1,0:T(8,128)(2,1)S(1)}, u32[]{:S(2)}, u32[]{:S(2)}) collective-permute-start(bf16[512,1024]{1,0:T(8,128)(2,1)S(1)} %collective-permute-done.14), channel_id=1, source_target_pairs={{0,1},{1,0},{2,3},{3,2},{4,5},{5,4},{6,7},{7,6},{8,9},{9,8},{10,11... | collective-permute-start | bytes 3145736 | tf_op jit(solution)/shard_map/ppermute | solution.py:30
  60.4 6.6 %collective-permute-start.15 = (bf16[128,512]{1,0:T(8,128)(2,1)S(1)}, bf16[128,512]{1,0:T(8,128)(2,1)S(1)}, u32[]{:S(2)}, u32[]{:S(2)}) collective-permute-start(bf16[128,512]{1,0:T(8,128)(2,1)S(1)} %merge.1), channel_id=1, source_target_pairs={{0,128},{64,192},{128,0},{192,64},{1,129},{65,193},{129,1},{193,65... | collective-permute-start | bytes 393224 | tf_op jit(solution)/shard_map/ppermute | solution.py:30
  61.2 6.2 %collective-permute-start.16 = (bf16[128,512]{1,0:T(8,128)(2,1)S(1)}, bf16[128,512]{1,0:T(8,128)(2,1)S(1)}, u32[]{:S(2)}, u32[]{:S(2)}) collective-permute-start(bf16[128,512]{1,0:T(8,128)(2,1)S(1)} %merge.1), channel_id=1, source_target_pairs={{0,32},{2,34},{32,0},{34,2},{1,33},{3,35},{33,1},{35,3},{4,36},{6,... | collective-permute-start | bytes 393224 | tf_op jit(solution)/shard_map/ppermute | solution.py:30
  61.2 10.9 %collective-permute-start.17 = (bf16[128,512]{1,0:T(8,128)(2,1)S(1)}, bf16[128,512]{1,0:T(8,128)(2,1)S(1)}, u32[]{:S(2)}, u32[]{:S(2)}) collective-permute-start(bf16[128,512]{1,0:T(8,128)(2,1)S(1)} %merge.1), channel_id=1, source_target_pairs={{0,160},{32,128},{128,32},{160,0},{1,161},{33,129},{129,33},{161,1... | collective-permute-start | bytes 393224 | tf_op jit(solution)/shard_map/ppermute | solution.py:546
  77.7 8.4 %collective-permute-start.33 = (bf16[32,1024]{1,0:T(8,128)(2,1)S(1)}, bf16[32,1024]{1,0:T(8,128)(2,1)S(1)}, u32[]{:S(2)}, u32[]{:S(2)}) collective-permute-start(bf16[32,1024]{1,0:T(8,128)(2,1)S(1)} %get-tuple-element.84), channel_id=1, source_target_pairs={{0,28},{4,0},{8,4},{12,8},{16,12},{20,16},{24,20},{28,24},{1,29},{... | collective-permute-start | bytes 196616 | tf_op jit(solution)/shard_map/ppermute | solution.py:30
  83.4 5.6 %collective-permute-start.25 = (bf16[32,1024]{1,0:T(8,128)(2,1)S(1)}, bf16[32,1024]{1,0:T(8,128)(2,1)S(1)}, u32[]{:S(2)}, u32[]{:S(2)}) collective-permute-start(bf16[32,1024]{1,0:T(8,128)(2,1)S(1)} %get-tuple-element.75), channel_id=1, source_target_pairs={{0,28},{4,0},{8,4},{12,8},{16,12},{20,16},{24,20},{28,24},{1,29},{... | collective-permute-start | bytes 196616 | tf_op jit(solution)/shard_map/ppermute | solution.py:30
  86.1 5.7 %collective-permute-start.21 = (bf16[32,1024]{1,0:T(8,128)(2,1)S(1)}, bf16[32,1024]{1,0:T(8,128)(2,1)S(1)}, u32[]{:S(2)}, u32[]{:S(2)}) collective-permute-start(bf16[32,1024]{1,0:T(8,128)(2,1)S(1)} %get-tuple-element.71), channel_id=1, source_target_pairs={{0,4},{4,8},{8,12},{12,16},{16,20},{20,24},{24,28},{28,0},{1,5},{5... | collective-permute-start | bytes 196616 | tf_op jit(solution)/shard_map/ppermute | solution.py:30
  86.2 5.8 %collective-permute-start.34 = (bf16[64,1024]{1,0:T(8,128)(2,1)S(1)}, bf16[64,1024]{1,0:T(8,128)(2,1)S(1)}, u32[]{:S(2)}, u32[]{:S(2)}) collective-permute-start(bf16[64,1024]{1,0:T(8,128)(2,1)S(1)} %pad_maximum_fusion.3), channel_id=1, source_target_pairs={{0,28},{4,0},{8,4},{12,8},{16,12},{20,16},{24,20},{28,24},{1,29},{... | collective-permute-start | bytes 393224 | tf_op jit(solution)/shard_map/ppermute | solution.py:30
  88.9 5.8 %collective-permute-start.30 = (bf16[64,1024]{1,0:T(8,128)(2,1)S(1)}, bf16[64,1024]{1,0:T(8,128)(2,1)S(1)}, u32[]{:S(2)}, u32[]{:S(2)}) collective-permute-start(bf16[64,1024]{1,0:T(8,128)(2,1)S(1)} %pad_maximum_fusion.2), channel_id=1, source_target_pairs={{0,4},{4,8},{8,12},{12,16},{16,20},{20,24},{24,28},{28,0},{1,5},{5... | collective-permute-start | bytes 393224 | tf_op jit(solution)/shard_map/ppermute | solution.py:30
  89.1 5.8 %collective-permute-start.26 = (bf16[64,1024]{1,0:T(8,128)(2,1)S(1)}, bf16[64,1024]{1,0:T(8,128)(2,1)S(1)}, u32[]{:S(2)}, u32[]{:S(2)}) collective-permute-start(bf16[64,1024]{1,0:T(8,128)(2,1)S(1)} %pad_maximum_fusion.1), channel_id=1, source_target_pairs={{0,28},{4,0},{8,4},{12,8},{16,12},{20,16},{24,20},{28,24},{1,29},{... | collective-permute-start | bytes 393224 | tf_op jit(solution)/shard_map/ppermute | solution.py:30
  91.9 5.8 %collective-permute-start.22 = (bf16[64,1024]{1,0:T(8,128)(2,1)S(1)}, bf16[64,1024]{1,0:T(8,128)(2,1)S(1)}, u32[]{:S(2)}, u32[]{:S(2)}) collective-permute-start(bf16[64,1024]{1,0:T(8,128)(2,1)S(1)} %pad_maximum_fusion), channel_id=1, source_target_pairs={{0,4},{4,8},{8,12},{12,16},{16,20},{20,24},{24,28},{28,0},{1,5},{5... | collective-permute-start | bytes 393224 | tf_op jit(solution)/shard_map/ppermute | solution.py:30
  92.0 5.8 %collective-permute-start.35 = (bf16[64,1024]{1,0:T(8,128)(2,1)S(1)}, bf16[64,1024]{1,0:T(8,128)(2,1)S(1)}, u32[]{:S(2)}, u32[]{:S(2)}) collective-permute-start(bf16[64,1024]{1,0:T(8,128)(2,1)S(1)} %add_convert_fusion.1), channel_id=1, source_target_pairs={{0,28},{4,0},{8,4},{12,8},{16,12},{20,16},{24,20},{28,24},{1,29},{... | collective-permute-start | bytes 393224 | tf_op jit(solution)/shard_map/ppermute | solution.py:30
  94.8 6.6 %collective-permute-start.31 = (bf16[64,1024]{1,0:T(8,128)(2,1)S(1)}, bf16[64,1024]{1,0:T(8,128)(2,1)S(1)}, u32[]{:S(2)}, u32[]{:S(2)}) collective-permute-start(bf16[64,1024]{1,0:T(8,128)(2,1)S(1)} %add_convert_fusion.3), channel_id=1, source_target_pairs={{0,4},{4,8},{8,12},{12,16},{16,20},{20,24},{24,28},{28,0},{1,5},{5... | collective-permute-start | bytes 393224 | tf_op jit(solution)/shard_map/ppermute | solution.py:30
  94.9 6.5 %collective-permute-start.27 = (bf16[64,1024]{1,0:T(8,128)(2,1)S(1)}, bf16[64,1024]{1,0:T(8,128)(2,1)S(1)}, u32[]{:S(2)}, u32[]{:S(2)}) collective-permute-start(bf16[64,1024]{1,0:T(8,128)(2,1)S(1)} %add_convert_fusion.5), channel_id=1, source_target_pairs={{0,28},{4,0},{8,4},{12,8},{16,12},{20,16},{24,20},{28,24},{1,29},{... | collective-permute-start | bytes 393224 | tf_op jit(solution)/shard_map/ppermute | solution.py:30
  97.7 6.6 %collective-permute-start.23 = (bf16[64,1024]{1,0:T(8,128)(2,1)S(1)}, bf16[64,1024]{1,0:T(8,128)(2,1)S(1)}, u32[]{:S(2)}, u32[]{:S(2)}) collective-permute-start(bf16[64,1024]{1,0:T(8,128)(2,1)S(1)} %add_convert_fusion.7), channel_id=1, source_target_pairs={{0,4},{4,8},{8,12},{12,16},{16,20},{20,24},{24,28},{28,0},{1,5},{5... | collective-permute-start | bytes 393224 | tf_op jit(solution)/shard_map/ppermute | solution.py:30
  97.9 6.6 %collective-permute-start.36 = (bf16[64,1024]{1,0:T(8,128)(2,1)S(1)}, bf16[64,1024]{1,0:T(8,128)(2,1)S(1)}, u32[]{:S(2)}, u32[]{:S(2)}) collective-permute-start(bf16[64,1024]{1,0:T(8,128)(2,1)S(1)} %add_convert_fusion), channel_id=1, source_target_pairs={{0,28},{4,0},{8,4},{12,8},{16,12},{20,16},{24,20},{28,24},{1,29},{... | collective-permute-start | bytes 393224 | tf_op jit(solution)/shard_map/ppermute | solution.py:30
  101.4 6.0 %collective-permute-start.32 = (bf16[64,1024]{1,0:T(8,128)(2,1)S(1)}, bf16[64,1024]{1,0:T(8,128)(2,1)S(1)}, u32[]{:S(2)}, u32[]{:S(2)}) collective-permute-start(bf16[64,1024]{1,0:T(8,128)(2,1)S(1)} %add_convert_fusion.2), channel_id=1, source_target_pairs={{0,4},{4,8},{8,12},{12,16},{16,20},{20,24},{24,28},{28,0},{1,5},{5... | collective-permute-start | bytes 393224 | tf_op jit(solution)/shard_map/ppermute | solution.py:30
  101.5 5.8 %collective-permute-start.28 = (bf16[64,1024]{1,0:T(8,128)(2,1)S(1)}, bf16[64,1024]{1,0:T(8,128)(2,1)S(1)}, u32[]{:S(2)}, u32[]{:S(2)}) collective-permute-start(bf16[64,1024]{1,0:T(8,128)(2,1)S(1)} %add_convert_fusion.4), channel_id=1, source_target_pairs={{0,28},{4,0},{8,4},{12,8},{16,12},{20,16},{24,20},{28,24},{1,29},{... | collective-permute-start | bytes 393224 | tf_op jit(solution)/shard_map/ppermute | solution.py:30
  (10 other events, 135.3 us)
where the time goes:
time: 129 us; the launch traced here: 130 us
  starting transfers between devices  56.7 us (44%)
  Pallas kernels  26.9 us (21%)
  waiting for transfers between devices  26.2 us (20%)
  blocking collectives  18.7 us (14%)
    ppermute x34, starting transfers between devices, moved(): lax.ppermute(value, axis, [(i, (i + step) % size) for i in range(size)])  48.8 us
    ppermute x34, waiting for transfers between devices, moved(): lax.ppermute(value, axis, [(i, (i + step) % size) for i in range(size)])  21.5 us
    all_to_all x1, blocking collectives, shards(): lax.all_to_all(blocks, ('yp', 'xh', 'xl', 'core'), 0, 0, tiled=True)  18.7 us
    pallas_call x2, Pallas kernels, attend(): pl.pallas_call(lambda *refs: attend_body(first, last, sources, *refs), ou...  17.5 us
    ppermute x1, starting transfers between devices, shards(): lax.ppermute(attended, ('yp', 'xh'), [(i, 3 - i) for i in range(4)])  4.98 us
    ppermute x1, waiting for transfers between devices, shards(): lax.ppermute(attended, ('yp', 'xh'), [(i, 3 - i) for i in range(4)])  4.72 us
    ppermute x2, starting transfers between devices, to_y_pair(): return lax.ppermute(value, ('yp', 'yl', 'core'), pairs)  2.97 us
    pallas_call x1, Pallas kernels, halves(): pl.pallas_call(halves_body, out_shape=[jax.ShapeDtypeStruct((weight.shape...  2.9 us
  transfers between devices with their start and end apart: 37, of which 13 were waited for; matrix products, arithmetic and copies ran while one was open for 0% of the time, Pallas kernels for 16%

commit v1 on v0

--- a/solution.py
+++ b/solution.py
@@ -34,12 +34,13 @@
     return moved(value, ("yp", "yl"), 4, step)
 
 
-def to_y_pair(value, flip):
+def to_y_pair(value, swap):
     pairs = []
     for y in range(4):
         for core in range(2):
-            other = y ^ 1 if core == flip else (y + (1 if y % 2 else 3)) % 4
-            pairs.append((y * 2 + core, other * 2 + core))
+            there = 1 - core if swap else core
+            other = y ^ 1 if there == 0 else (y + (1 if y % 2 else 3)) % 4
+            pairs.append((y * 2 + core, other * 2 + there))
     return lax.ppermute(value, ("yp", "yl", "core"), pairs)
 
 
@@ -141,9 +142,9 @@
     )(weight)
 
 
-def update(s, values_t, cols, m_ref, acc_ref):
+def update(s, top, values_t, cols, m_ref, acc_ref):
     old = m_ref[:, cols]
-    new = jnp.maximum(old, jnp.max(s, axis=0, keepdims=True))
+    new = jnp.maximum(old, top)
     p = jnp.exp2(s - new).astype(BF16)
     m_ref[:, cols] = new
     acc_ref[:, cols] = acc_ref[:, cols] * jnp.exp2(old - new) + jnp.dot(
@@ -151,7 +152,7 @@
     )
 
 
-def flash(block_count, base_ref, keys2, values_t, rows_t, m_ref, acc_ref, s_ref):
+def flash(block_count, base_ref, keys2, values_t, rows_t, m_ref, acc_ref, s_ref, top_ref):
     def place(step):
         cols = pl.multiple_of((step % HEADS) * HEAD_ROWS, HEAD_ROWS)
         base = pl.multiple_of(base_ref[step // HEADS], BLOCK)
@@ -159,11 +160,13 @@
 
     def score(step, slot):
         at, cols = place(step)
-        s_ref[slot] = jnp.dot(keys2[at, :], rows_t[:, cols], preferred_element_type=F32)
+        s = jnp.dot(keys2[at, :], rows_t[:, cols], preferred_element_type=F32)
+        s_ref[slot] = s
+        top_ref[slot] = jnp.max(s, axis=0, keepdims=True)
 
     def settle(step, slot):
         at, cols = place(step)
-        update(s_ref[slot], values_t[:, at], cols, m_ref, acc_ref)
+        update(s_ref[slot], top_ref[slot], values_t[:, at], cols, m_ref, acc_ref)
 
     steps = block_count * HEADS
 
@@ -207,7 +210,8 @@
     for head in range(HEADS):
         following = score(head + 1) if head + 1 < HEADS else None
         cols = slice(head * HEAD_ROWS, (head + 1) * HEAD_ROWS)
-        update(s, values_t, cols, m_ref, acc_ref)
+        top = jnp.max(s, axis=0, keepdims=True)
+        update(s, top, values_t, cols, m_ref, acc_ref)
         s = following
 
 
@@ -230,7 +234,7 @@
         m_ref, acc_ref = refs.pop(0), refs.pop(0)
     else:
         m_ref, acc_ref = m_out, acc_out
-    keys2, values_t, base_ref, s_ref = refs
+    keys2, values_t, base_ref, s_ref, top_ref = refs
 
     if first:
         for i, q_ref in enumerate(q_refs):
@@ -281,7 +285,7 @@
     else:
         absorb_fresh(carry_in, kv_refs, rows_t, row_pos, m_ref, acc_ref)
 
-    flash(block_count, base_ref, keys2, values_t, rows_t, m_ref, acc_ref, s_ref)
+    flash(block_count, base_ref, keys2, values_t, rows_t, m_ref, acc_ref, s_ref, top_ref)
 
     if last:
         for i, out_ref in enumerate(out_refs):
@@ -323,6 +327,7 @@
         pltpu.VMEM((VROWS, slots), BF16),
         pltpu.SMEM((slots // BLOCK + 1,), jnp.int32),
         pltpu.VMEM((2, BLOCK, HEAD_ROWS), F32),
+        pltpu.VMEM((2, 1, HEAD_ROWS), F32),
     ]
     return pl.pallas_call(
         lambda *refs: attend_body(first, last, sources, *refs),
@@ -371,14 +376,12 @@
 
 def project_body(*refs):
     x_own, x_other = refs[0:2]
-    weights = refs[2:6]
-    outs = refs[6:24]
-    x_ref, w_ref, sems = refs[24:27]
+    weights = refs[2:4]
+    out = refs[4:13]
+    x_ref, w_ref, sems = refs[13:16]
     depth = weights[0].shape[0]
     copies = [
-        pltpu.make_async_copy(
-            weight, w_ref.at[i // 2, pl.ds((i % 2) * depth, depth)], sems.at[i]
-        )
+        pltpu.make_async_copy(weight, w_ref.at[pl.ds(i * depth, depth)], sems.at[i])
         for i, weight in enumerate(weights)
     ]
     for copy in copies:
@@ -393,38 +396,35 @@
             x_ref[row : row + 16, depth : 2 * depth] = x_other[source, :]
     for copy in copies:
         copy.wait()
-    for side in range(2):
-        out = outs[side * 9 : side * 9 + 9]
-        for n in range(4):
-            cols = slice(n * 256, (n + 1) * 256)
-            y = jnp.dot(x_ref[...], w_ref[side, :, cols], preferred_element_type=F32).astype(BF16)
-            for r in range(8):
-                if r < 4:
-                    out[r][:, cols] = y[r * 64 : (r + 1) * 64]
-                elif r == 4:
-                    out[4][:, cols] = y[256:288]
-                    out[5][:, cols] = y[288:320]
-                else:
-                    out[r + 1][:, cols] = y[r * 64 : (r + 1) * 64]
+    for n in range(4):
+        cols = slice(n * 256, (n + 1) * 256)
+        y = jnp.dot(x_ref[...], w_ref[:, cols], preferred_element_type=F32).astype(BF16)
+        for r in range(8):
+            if r < 4:
+                out[r][:, cols] = y[r * 64 : (r + 1) * 64]
+            elif r == 4:
+                out[4][:, cols] = y[256:288]
+                out[5][:, cols] = y[288:320]
+            else:
+                out[r + 1][:, cols] = y[r * 64 : (r + 1) * 64]
 
 
 def project(x_own, x_other, weights):
     full = jax.ShapeDtypeStruct((64, WIDE), BF16)
     half = jax.ShapeDtypeStruct((32, WIDE), BF16)
-    outs = pl.pallas_call(
+    return pl.pallas_call(
         project_body,
-        out_shape=([full] * 4 + [half] * 2 + [full] * 3) * 2,
-        in_specs=[VMEM] * 2 + [HBM] * 4,
-        out_specs=[VMEM] * 18,
+        out_shape=[full] * 4 + [half] * 2 + [full] * 3,
+        in_specs=[VMEM] * 2 + [HBM] * 2,
+        out_specs=[VMEM] * 9,
         scratch_shapes=[
             pltpu.VMEM((512, 1024), BF16),
-            pltpu.VMEM((2, 1024, WIDE), BF16),
-            pltpu.SemaphoreType.DMA((4,)),
+            pltpu.VMEM((1024, WIDE), BF16),
+            pltpu.SemaphoreType.DMA((2,)),
         ],
-        compiler_params=params(16),
+        compiler_params=params(12),
         name="project",
     )(x_own, x_other, *weights)
-    return outs[:9], outs[9:]
 
 
 def sum_bf16(a, b):
@@ -515,7 +515,7 @@
     q_all = (q_prev, q_next, q_far)
     w_kept, w_away = halves(after(out_weight, q_prev))
     other = to_other_core(after(kv, q_all))
-    w_kept_pair, w_away_pair = to_y_pair(w_kept, 0), to_y_pair(w_away, 1)
+    w_kept_pair, w_other_pair = to_y_pair(w_kept, False), to_y_pair(w_away, True)
     left, right = after((left, right), w_kept)
     far = along_x(after(kv, (left, right)), 2)
     rows_t, row_pos, m, acc, carry = attend(
@@ -538,16 +538,17 @@
     )
     attended = merge((mine, along_y(prev, -1), along_y(following, 1), along_y(distant, 2)))
 
-    attended, w_kept_pair, w_away_pair = lax.optimization_barrier(
-        (attended, w_kept_pair, w_away_pair)
-    )
-    w_other, w_other_pair = to_other_core(w_away), to_other_core(w_away_pair)
+    attended, w_kept_pair, w_other_pair = lax.optimization_barrier(
+        (attended, w_kept_pair, w_other_pair)
+    )
+    w_other = to_other_core(w_away)
 
     corner = lax.ppermute(attended, ("yp", "xh"), [(i, 3 - i) for i in range(4)])
     blocks = (attended, along_y(attended, 2), along_x(attended, 2), corner)
     x_own = jnp.concatenate(blocks, axis=0)
-    weights = (w_kept, w_other, w_kept_pair, w_other_pair)
-    near, pair = project(x_own, to_other_core(x_own), weights)
+    x_other = to_other_core(x_own)
+    near = project(x_own, x_other, (w_kept, w_other))
+    pair = project(x_own, x_other, (w_kept_pair, w_other_pair))
     blocks = ordered((*sum_over_z(near), *sum_over_z(pair))).reshape(64, 2 * WIDE)
     spread = lax.all_to_all(blocks, ("yp", "xh", "xl", "core"), 0, 0, tiled=True)
     return finish(spread)

time: 129 us -> 132 us (1.023)
  Pallas kernels: 26.9 us -> 19.6 us
  starting transfers between devices: 56.7 us -> 61.7 us
  waiting for transfers between devices: 26.2 us -> 30.9 us
    pallas_call x2, Pallas kernels: 17.5 us -> 10 us  [attend(): pl.pallas_call(lambda *refs: attend_body(first, last, sources, *refs), ou...]
    ppermute x34 -> x33, waiting for transfers between devices: 21.5 us -> 26.9 us  [moved(): lax.ppermute(value, axis, [(i, (i + step) % size) for i in range(size)])]
    ppermute x34 -> x33, starting transfers between devices: 48.8 us -> 53.9 us  [moved(): lax.ppermute(value, axis, [(i, (i + step) % size) for i in range(size)])]
    pallas_call x1 -> x2, Pallas kernels: 2.74 us -> 2.98 us  [project(): pl.pallas_call(project_body, out_shape=[full] * 4 + [half] * 2 + [full] *...]
  transfers between devices with their start and end apart: 37 -> 36, of which waited for: 13 -> 12; matrix products, arithmetic and copies ran while one was open for 0% -> 0% of each run, Pallas kernels for 16% -> 12%
where the time goes in v1:
time: 132 us; the launch traced here: 131 us
  starting transfers between devices  61.7 us (47%)
  waiting for transfers between devices  30.9 us (23%)
  Pallas kernels  19.6 us (15%)
  blocking collectives  18.1 us (14%)
    ppermute x33, starting transfers between devices, moved(): lax.ppermute(value, axis, [(i, (i + step) % size) for i in range(size)])  53.9 us
    ppermute x33, waiting for transfers between devices, moved(): lax.ppermute(value, axis, [(i, (i + step) % size) for i in range(size)])  26.9 us
    all_to_all x1, blocking collectives, shards(): lax.all_to_all(blocks, ('yp', 'xh', 'xl', 'core'), 0, 0, tiled=True)  18.1 us
    pallas_call x2, Pallas kernels, attend(): pl.pallas_call(lambda *refs: attend_body(first, last, sources, *refs), ou...  10 us
    ppermute x1, waiting for transfers between devices, shards(): lax.ppermute(attended, ('yp', 'xh'), [(i, 3 - i) for i in range(4)])  4.01 us
    ppermute x2, starting transfers between devices, to_y_pair(): return lax.ppermute(value, ('yp', 'yl', 'core'), pairs)  4.01 us
    ppermute x1, starting transfers between devices, shards(): lax.ppermute(attended, ('yp', 'xh'), [(i, 3 - i) for i in range(4)])  3.75 us
    pallas_call x2, Pallas kernels, project(): pl.pallas_call(project_body, out_shape=[full] * 4 + [half] * 2 + [full] *...  2.98 us
  transfers between devices with their start and end apart: 36, of which 12 were waited for; matrix products, arithmetic and copies ran while one was open for 0% of the time, Pallas kernels for 12%

profile of v1, /device:TPU:1, one launch (start us, length us, event | category | flops | bytes accessed | tf_op | source)
XLA Modules:
  0.0 131.4 jit_solution(18429845548808215555)
XLA Ops:
  0.0 2.7 %pack.1 = (bf16[144,512]{1,0:T(8,128)(2,1)}, bf16[2176,128]{1,0:T(8,128)(2,1)}) custom-call(bf16[128,512]{1,0:T(8,128)(2,1)} %q_hbm.1, bf16[1024,128]{1,0:T(8,128)(2,1)} %bitcast.3, bf16[1024,128]{1,0:T(8,128)(2,1)} %bitcast.4, bf16[128,1024]{1,0:T(8,128)(2,1)} %nk_hbm.1, bf16[128,1024]{1,0:T(8,128)(2,1)} %nv_hbm.1, s32[1,128]{1,0:T(1,128)} %bitcast.5), custom_call_target="tpu_custom_call" | custom-call | tf_op jit(solution)/shard_map/pack/pallas_call | solution.py:107
  2.7 2.1 %collective-permute-start.4 = (bf16[2176,128]{1,0:T(8,128)(2,1)}, bf16[2176,128]{1,0:T(8,128)(2,1)S(1)}, u32[]{:S(2)}, u32[]{:S(2)}) collective-permute-start(bf16[2176,128]{1,0:T(8,128)(2,1)} %get-tuple-element.57.refs_5_), channel_id=1, source_target_pairs={{0,2},{2,32},{32,34},{34,0},{1,3},{3,33},{33,35},{35,1},{4,6},{6,3... | collective-permute-start | bytes 1671176 | tf_op jit(solution)/shard_map/ppermute | solution.py:30
  9.0 1.6 %collective-permute-start.2 = (bf16[144,512]{1,0:T(8,128)(2,1)}, bf16[144,512]{1,0:T(8,128)(2,1)S(1)}, u32[]{:S(2)}, u32[]{:S(2)}) collective-permute-start(bf16[144,512]{1,0:T(8,128)(2,1)} %get-tuple-element.45.refs_1_), channel_id=1, source_target_pairs={{0,128},{64,192},{128,0},{192,64},{1,129},{65,193},{129,1},{193,65... | collective-permute-start | bytes 442376 | tf_op jit(solution)/shard_map/ppermute | solution.py:30
  12.1 2.9 %halves.1 = (bf16[512,1024]{1,0:T(8,128)(2,1)}, bf16[512,1024]{1,0:T(8,128)(2,1)}) custom-call(bf16[512,2048]{1,0:T(8,128)(2,1)} %w_hbm), custom_call_target="tpu_custom_call" | custom-call | tf_op jit(solution)/shard_map/halves/pallas_call | solution.py:135
  16.3 3.9 %collective-permute-start.3 = (bf16[2176,128]{1,0:T(8,128)(2,1)S(1)}, bf16[2176,128]{1,0:T(8,128)(2,1)S(1)}, u32[]{:S(2)}, u32[]{:S(2)}) collective-permute-start(bf16[2176,128]{1,0:T(8,128)(2,1)S(1)} %copy-done.1), channel_id=1, source_target_pairs={{0,1},{1,0},{2,3},{3,2},{4,5},{5,4},{6,7},{7,6},{8,9},{9,8},{10,11... | collective-permute-start | bytes 1671176 | tf_op jit(solution)/shard_map/ppermute | solution.py:30
  20.4 3.0 %collective-permute-start.13 = (bf16[512,1024]{1,0:T(8,128)(2,1)}, bf16[512,1024]{1,0:T(8,128)(2,1)S(1)}, u32[]{:S(2)}, u32[]{:S(2)}) collective-permute-start(bf16[512,1024]{1,0:T(8,128)(2,1)} %get-tuple-element.49.refs_2_), channel_id=1, source_target_pairs={{0,64},{1,193},{64,0},{65,129},{128,192},{129,65},{192,128},{193,1... | collective-permute-start | bytes 3145736 | tf_op jit(solution)/shard_map/ppermute | solution.py:44
  25.0 4.6 %attend.2 = (bf16[256,2048]{1,0:T(8,128)(2,1)S(1)}, f32[1,512]{1,0:T(1,128)S(1)}, f32[1,2048]{1,0:T(1,128)S(1)}, f32[144,2048]{1,0:T(8,128)S(1)}, bf16[512,128]{1,0:T(8,128)(2,1)S(1)}) custom-call(s32[8]{0:T(128)S(1)} %copy-done.3, bf16[144,512]{1,0:T(8,128)(2,1)S(1)} %copy-done.2, bf16[144,512]{1,0:T(8,128)(2,1)S(1)} %collective-permute-done.refs_2_, ...), custom_call_target="tpu_custom_call" | custom-call | flops 1000000 | bytes 1024 | tf_op jit(solution)/shard_map/attend/pallas_call | solution.py:332
  29.6 6.4 %collective-permute-done.8.refs_8_ = bf16[2176,128]{1,0:T(8,128)(2,1)S(1)} collective-permute-done((bf16[2176,128]{1,0:T(8,128)(2,1)S(1)}, bf16[2176,128]{1,0:T(8,128)(2,1)S(1)}, u32[]{:S(2)}, u32[]{:S(2)}) %collective-permute-start.8) | collective-permute-done | bytes 557088 | tf_op jit(solution)/shard_map/ppermute | solution.py:30
  36.8 1.6 %collective-permute-done.9.refs_9_ = bf16[2176,128]{1,0:T(8,128)(2,1)S(1)} collective-permute-done((bf16[2176,128]{1,0:T(8,128)(2,1)S(1)}, bf16[2176,128]{1,0:T(8,128)(2,1)S(1)}, u32[]{:S(2)}, u32[]{:S(2)}) %collective-permute-start.9) | collective-permute-done | bytes 557088 | tf_op jit(solution)/shard_map/ppermute | solution.py:30
  38.4 5.4 %attend.3 = (bf16[528,128]{1,0:T(8,128)(2,1)S(1)}, bf16[528,128]{1,0:T(8,128)(2,1)S(1)}, bf16[528,128]{1,0:T(8,128)(2,1)S(1)}, bf16[528,128]{1,0:T(8,128)(2,1)S(1)}) custom-call(s32[8]{0:T(128)S(1)} %copy-done.3, bf16[256,2048]{1,0:T(8,128)(2,1)S(1)} %get-tuple-element.52.refs_1_, f32[1,512]{1,0:T(1,128)S(1)} %get-tuple-element.53.refs_2_, ...), custom_call_target="tpu_custom_call" | custom-call | flops 1000000 | bytes 1024 | tf_op jit(solution)/shard_map/attend/pallas_call | solution.py:332
  43.8 5.8 %collective-permute-start.10 = (bf16[528,128]{1,0:T(8,128)(2,1)S(1)}, bf16[528,128]{1,0:T(8,128)(2,1)S(1)}, u32[]{:S(2)}, u32[]{:S(2)}) collective-permute-start(bf16[528,128]{1,0:T(8,128)(2,1)S(1)} %get-tuple-element.60), channel_id=1, source_target_pairs={{0,192},{64,0},{128,64},{192,128},{1,193},{65,1},{129,65},{193,129... | collective-permute-start | bytes 405512 | tf_op jit(solution)/shard_map/ppermute | solution.py:30
  49.6 3.0 %collective-permute-start.11 = (bf16[528,128]{1,0:T(8,128)(2,1)S(1)}, bf16[528,128]{1,0:T(8,128)(2,1)S(1)}, u32[]{:S(2)}, u32[]{:S(2)}) collective-permute-start(bf16[528,128]{1,0:T(8,128)(2,1)S(1)} %get-tuple-element.61), channel_id=1, source_target_pairs={{0,64},{64,128},{128,192},{192,0},{1,65},{65,129},{129,193},{193,1... | collective-permute-start | bytes 405512 | tf_op jit(solution)/shard_map/ppermute | solution.py:30
  52.6 1.7 %collective-permute-start.12 = (bf16[528,128]{1,0:T(8,128)(2,1)S(1)}, bf16[528,128]{1,0:T(8,128)(2,1)S(1)}, u32[]{:S(2)}, u32[]{:S(2)}) collective-permute-start(bf16[528,128]{1,0:T(8,128)(2,1)S(1)} %get-tuple-element.62), channel_id=1, source_target_pairs={{0,128},{64,192},{128,0},{192,64},{1,129},{65,193},{129,1},{193,65... | collective-permute-start | bytes 405512 | tf_op jit(solution)/shard_map/ppermute | solution.py:30
  54.3 2.0 %collective-permute-done.10.refs_1_ = bf16[528,128]{1,0:T(8,128)(2,1)S(1)} collective-permute-done((bf16[528,128]{1,0:T(8,128)(2,1)S(1)}, bf16[528,128]{1,0:T(8,128)(2,1)S(1)}, u32[]{:S(2)}, u32[]{:S(2)}) %collective-permute-start.10) | collective-permute-done | bytes 135200 | tf_op jit(solution)/shard_map/ppermute | solution.py:30
  56.3 4.4 %collective-permute-done.12.refs_3_ = bf16[528,128]{1,0:T(8,128)(2,1)S(1)} collective-permute-done((bf16[528,128]{1,0:T(8,128)(2,1)S(1)}, bf16[528,128]{1,0:T(8,128)(2,1)S(1)}, u32[]{:S(2)}, u32[]{:S(2)}) %collective-permute-start.12) | collective-permute-done | bytes 135200 | tf_op jit(solution)/shard_map/ppermute | solution.py:30
  64.3 3.8 %collective-permute-start.17 = (bf16[128,512]{1,0:T(8,128)(2,1)S(1)}, bf16[128,512]{1,0:T(8,128)(2,1)S(1)}, u32[]{:S(2)}, u32[]{:S(2)}) collective-permute-start(bf16[128,512]{1,0:T(8,128)(2,1)S(1)} %merge.1), channel_id=1, source_target_pairs={{0,160},{32,128},{128,32},{160,0},{1,161},{33,129},{129,33},{161,1... | collective-permute-start | bytes 393224 | tf_op jit(solution)/shard_map/ppermute | solution.py:546
  68.1 2.3 %collective-permute-done.16 = bf16[128,512]{1,0:T(8,128)(2,1)S(1)} collective-permute-done((bf16[128,512]{1,0:T(8,128)(2,1)S(1)}, bf16[128,512]{1,0:T(8,128)(2,1)S(1)}, u32[]{:S(2)}, u32[]{:S(2)}) %collective-permute-start.16) | collective-permute-done | bytes 131104 | tf_op jit(solution)/shard_map/ppermute | solution.py:30
  70.4 4.0 %collective-permute-done.17 = bf16[128,512]{1,0:T(8,128)(2,1)S(1)} collective-permute-done((bf16[128,512]{1,0:T(8,128)(2,1)S(1)}, bf16[128,512]{1,0:T(8,128)(2,1)S(1)}, u32[]{:S(2)}, u32[]{:S(2)}) %collective-permute-start.17) | collective-permute-done | bytes 131104 | tf_op jit(solution)/shard_map/ppermute | solution.py:546
  75.3 1.5 %collective-permute-done.18.refs_1_ = bf16[512,512]{1,0:T(8,128)(2,1)S(1)} collective-permute-done((bf16[512,512]{1,0:T(8,128)(2,1)S(1)}, bf16[512,512]{1,0:T(8,128)(2,1)S(1)}, u32[]{:S(2)}, u32[]{:S(2)}) %collective-permute-start.18) | collective-permute-done | bytes 524320 | tf_op jit(solution)/shard_map/ppermute | solution.py:30
  76.9 1.5 %project.3 = (bf16[64,1024]{1,0:T(8,128)(2,1)S(1)}, bf16[64,1024]{1,0:T(8,128)(2,1)S(1)}, bf16[64,1024]{1,0:T(8,128)(2,1)S(1)}, bf16[64,1024]{1,0:T(8,128)(2,1)S...) custom-call(bf16[512,512]{1,0:T(8,128)(2,1)S(1)} %constant_dynamic-u, ...), custom_call_target="tpu_custom_call" | custom-call | tf_op jit(solution)/shard_map/project/pallas_call | solution.py:415
  78.4 5.7 %collective-permute-start.32 = (bf16[32,1024]{1,0:T(8,128)(2,1)S(1)}, bf16[32,1024]{1,0:T(8,128)(2,1)S(1)}, u32[]{:S(2)}, u32[]{:S(2)}) collective-permute-start(bf16[32,1024]{1,0:T(8,128)(2,1)S(1)} %get-tuple-element.84), channel_id=1, source_target_pairs={{0,28},{4,0},{8,4},{12,8},{16,12},{20,16},{24,20},{28,24},{1,29},{... | collective-permute-start | bytes 196616 | tf_op jit(solution)/shard_map/ppermute | solution.py:30
  84.1 1.5 %project.2 = (bf16[64,1024]{1,0:T(8,128)(2,1)S(1)}, bf16[64,1024]{1,0:T(8,128)(2,1)S(1)}, bf16[64,1024]{1,0:T(8,128)(2,1)S(1)}, bf16[64,1024]{1,0:T(8,128)(2,1)S...) custom-call(bf16[512,512]{1,0:T(8,128)(2,1)S(1)} %constant_dynamic-u, ...), custom_call_target="tpu_custom_call" | custom-call | tf_op jit(solution)/shard_map/project/pallas_call | solution.py:415
  85.6 3.0 %collective-permute-start.24 = (bf16[32,1024]{1,0:T(8,128)(2,1)S(1)}, bf16[32,1024]{1,0:T(8,128)(2,1)S(1)}, u32[]{:S(2)}, u32[]{:S(2)}) collective-permute-start(bf16[32,1024]{1,0:T(8,128)(2,1)S(1)} %get-tuple-element.73), channel_id=1, source_target_pairs={{0,28},{4,0},{8,4},{12,8},{16,12},{20,16},{24,20},{28,24},{1,29},{... | collective-permute-start | bytes 196616 | tf_op jit(solution)/shard_map/ppermute | solution.py:30
  88.6 2.7 %collective-permute-start.33 = (bf16[64,1024]{1,0:T(8,128)(2,1)S(1)}, bf16[64,1024]{1,0:T(8,128)(2,1)S(1)}, u32[]{:S(2)}, u32[]{:S(2)}) collective-permute-start(bf16[64,1024]{1,0:T(8,128)(2,1)S(1)} %pad_maximum_fusion.3), channel_id=1, source_target_pairs={{0,28},{4,0},{8,4},{12,8},{16,12},{20,16},{24,20},{28,24},{1,29},{... | collective-permute-start | bytes 393224 | tf_op jit(solution)/shard_map/ppermute | solution.py:30
  91.5 2.7 %collective-permute-start.25 = (bf16[64,1024]{1,0:T(8,128)(2,1)S(1)}, bf16[64,1024]{1,0:T(8,128)(2,1)S(1)}, u32[]{:S(2)}, u32[]{:S(2)}) collective-permute-start(bf16[64,1024]{1,0:T(8,128)(2,1)S(1)} %pad_maximum_fusion.1), channel_id=1, source_target_pairs={{0,28},{4,0},{8,4},{12,8},{16,12},{20,16},{24,20},{28,24},{1,29},{... | collective-permute-start | bytes 393224 | tf_op jit(solution)/shard_map/ppermute | solution.py:30
  94.4 2.7 %collective-permute-start.34 = (bf16[64,1024]{1,0:T(8,128)(2,1)S(1)}, bf16[64,1024]{1,0:T(8,128)(2,1)S(1)}, u32[]{:S(2)}, u32[]{:S(2)}) collective-permute-start(bf16[64,1024]{1,0:T(8,128)(2,1)S(1)} %add_convert_fusion.1), channel_id=1, source_target_pairs={{0,28},{4,0},{8,4},{12,8},{16,12},{20,16},{24,20},{28,24},{1,29},{... | collective-permute-start | bytes 393224 | tf_op jit(solution)/shard_map/ppermute | solution.py:30
  97.4 2.7 %collective-permute-start.26 = (bf16[64,1024]{1,0:T(8,128)(2,1)S(1)}, bf16[64,1024]{1,0:T(8,128)(2,1)S(1)}, u32[]{:S(2)}, u32[]{:S(2)}) collective-permute-start(bf16[64,1024]{1,0:T(8,128)(2,1)S(1)} %add_convert_fusion.5), channel_id=1, source_target_pairs={{0,28},{4,0},{8,4},{12,8},{16,12},{20,16},{24,20},{28,24},{1,29},{... | collective-permute-start | bytes 393224 | tf_op jit(solution)/shard_map/ppermute | solution.py:30
  100.3 3.0 %collective-permute-start.35 = (bf16[64,1024]{1,0:T(8,128)(2,1)S(1)}, bf16[64,1024]{1,0:T(8,128)(2,1)S(1)}, u32[]{:S(2)}, u32[]{:S(2)}) collective-permute-start(bf16[64,1024]{1,0:T(8,128)(2,1)S(1)} %add_convert_fusion), channel_id=1, source_target_pairs={{0,28},{4,0},{8,4},{12,8},{16,12},{20,16},{24,20},{28,24},{1,29},{... | collective-permute-start | bytes 393224 | tf_op jit(solution)/shard_map/ppermute | solution.py:30
  104.0 2.8 %collective-permute-start.27 = (bf16[64,1024]{1,0:T(8,128)(2,1)S(1)}, bf16[64,1024]{1,0:T(8,128)(2,1)S(1)}, u32[]{:S(2)}, u32[]{:S(2)}) collective-permute-start(bf16[64,1024]{1,0:T(8,128)(2,1)S(1)} %add_convert_fusion.4), channel_id=1, source_target_pairs={{0,28},{4,0},{8,4},{12,8},{16,12},{20,16},{24,20},{28,24},{1,29},{... | collective-permute-start | bytes 393224 | tf_op jit(solution)/shard_map/ppermute | solution.py:30
  106.9 2.9 %collective-permute-done.31.refs_4_ = bf16[64,1024]{1,0:T(8,128)(2,1)S(1)} collective-permute-done((bf16[64,1024]{1,0:T(8,128)(2,1)S(1)}, bf16[64,1024]{1,0:T(8,128)(2,1)S(1)}, u32[]{:S(2)}, u32[]{:S(2)}) %collective-permute-start.31) | collective-permute-done | bytes 131104 | tf_op jit(solution)/shard_map/ppermute | solution.py:30
  109.8 2.5 %collective-permute-done.23.refs_1_ = bf16[64,1024]{1,0:T(8,128)(2,1)S(1)} collective-permute-done((bf16[64,1024]{1,0:T(8,128)(2,1)S(1)}, bf16[64,1024]{1,0:T(8,128)(2,1)S(1)}, u32[]{:S(2)}, u32[]{:S(2)}) %collective-permute-start.23) | collective-permute-done | bytes 131104 | tf_op jit(solution)/shard_map/ppermute | solution.py:30
  112.5 18.1 %all_to_all.11 = bf16[16,4,2048]{2,1,0:T(4,128)(2,1)S(1)} all-to-all(bf16[16,4,2048]{2,1,0:T(4,128)(2,1)S(1)} %all_to_all.7), channel_id=1, replica_groups=mesh['yp'=2,'yl'=2,'xh'=2,'z'=8,'xl'=2,'core'=2] {'yp','xh','xl','core'}, dimensions={0} | all-to-all | bytes 524288 | tf_op jit(solution)/shard_map/all_to_all | solution.py:553
  (86 shorter events, 16.5 us)
Async XLA Ops:
  2.7 17.5 %collective-permute-start.4 = (bf16[2176,128]{1,0:T(8,128)(2,1)}, bf16[2176,128]{1,0:T(8,128)(2,1)S(1)}, u32[]{:S(2)}, u32[]{:S(2)}) collective-permute-start(bf16[2176,128]{1,0:T(8,128)(2,1)} %get-tuple-element.57.refs_5_), channel_id=1, source_target_pairs={{0,2},{2,32},{32,34},{34,0},{1,3},{3,33},{33,35},{35,1},{4,6},{6,3... | collective-permute-start | bytes 1671176 | tf_op jit(solution)/shard_map/ppermute | solution.py:30
  4.8 15.4 %collective-permute-start.5 = (bf16[2176,128]{1,0:T(8,128)(2,1)}, bf16[2176,128]{1,0:T(8,128)(2,1)S(1)}, u32[]{:S(2)}, u32[]{:S(2)}) collective-permute-start(bf16[2176,128]{1,0:T(8,128)(2,1)} %get-tuple-element.57.refs_5_), channel_id=1, source_target_pairs={{0,34},{2,0},{32,2},{34,32},{1,35},{3,1},{33,3},{35,33},{4,38},{6,... | collective-permute-start | bytes 1671176 | tf_op jit(solution)/shard_map/ppermute | solution.py:30
  6.2 5.9 %collective-permute-start = (bf16[144,512]{1,0:T(8,128)(2,1)}, bf16[144,512]{1,0:T(8,128)(2,1)S(1)}, u32[]{:S(2)}, u32[]{:S(2)}) collective-permute-start(bf16[144,512]{1,0:T(8,128)(2,1)} %get-tuple-element.45.refs_1_), channel_id=1, source_target_pairs={{0,64},{64,128},{128,192},{192,0},{1,65},{65,129},{129,193},{193,1... | collective-permute-start | bytes 442376 | tf_op jit(solution)/shard_map/ppermute | solution.py:30
  7.6 7.4 %collective-permute-start.1 = (bf16[144,512]{1,0:T(8,128)(2,1)}, bf16[144,512]{1,0:T(8,128)(2,1)S(1)}, u32[]{:S(2)}, u32[]{:S(2)}) collective-permute-start(bf16[144,512]{1,0:T(8,128)(2,1)} %get-tuple-element.45.refs_1_), channel_id=1, source_target_pairs={{0,192},{64,0},{128,64},{192,128},{1,193},{65,1},{129,65},{193,129... | collective-permute-start | bytes 442376 | tf_op jit(solution)/shard_map/ppermute | solution.py:30
  9.0 7.3 %collective-permute-start.2 = (bf16[144,512]{1,0:T(8,128)(2,1)}, bf16[144,512]{1,0:T(8,128)(2,1)S(1)}, u32[]{:S(2)}, u32[]{:S(2)}) collective-permute-start(bf16[144,512]{1,0:T(8,128)(2,1)} %get-tuple-element.45.refs_1_), channel_id=1, source_target_pairs={{0,128},{64,192},{128,0},{192,64},{1,129},{65,193},{129,1},{193,65... | collective-permute-start | bytes 442376 | tf_op jit(solution)/shard_map/ppermute | solution.py:30
  16.3 8.1 %collective-permute-start.3 = (bf16[2176,128]{1,0:T(8,128)(2,1)S(1)}, bf16[2176,128]{1,0:T(8,128)(2,1)S(1)}, u32[]{:S(2)}, u32[]{:S(2)}) collective-permute-start(bf16[2176,128]{1,0:T(8,128)(2,1)S(1)} %copy-done.1), channel_id=1, source_target_pairs={{0,1},{1,0},{2,3},{3,2},{4,5},{5,4},{6,7},{7,6},{8,9},{9,8},{10,11... | collective-permute-start | bytes 1671176 | tf_op jit(solution)/shard_map/ppermute | solution.py:30
  20.2 15.7 %collective-permute-start.8 = (bf16[2176,128]{1,0:T(8,128)(2,1)S(1)}, bf16[2176,128]{1,0:T(8,128)(2,1)S(1)}, u32[]{:S(2)}, u32[]{:S(2)}) collective-permute-start(bf16[2176,128]{1,0:T(8,128)(2,1)S(1)} %copy-done.1), channel_id=1, source_target_pairs={{0,32},{2,34},{32,0},{34,2},{1,33},{3,35},{33,1},{35,3},{4,36},{6,... | collective-permute-start | bytes 1671176 | tf_op jit(solution)/shard_map/ppermute | solution.py:30
  20.4 40.5 %collective-permute-start.13 = (bf16[512,1024]{1,0:T(8,128)(2,1)}, bf16[512,1024]{1,0:T(8,128)(2,1)S(1)}, u32[]{:S(2)}, u32[]{:S(2)}) collective-permute-start(bf16[512,1024]{1,0:T(8,128)(2,1)} %get-tuple-element.49.refs_2_), channel_id=1, source_target_pairs={{0,64},{1,193},{64,0},{65,129},{128,192},{129,65},{192,128},{193,1... | collective-permute-start | bytes 3145736 | tf_op jit(solution)/shard_map/ppermute | solution.py:44
  23.4 37.6 %collective-permute-start.14 = (bf16[512,1024]{1,0:T(8,128)(2,1)}, bf16[512,1024]{1,0:T(8,128)(2,1)S(1)}, u32[]{:S(2)}, u32[]{:S(2)}) collective-permute-start(bf16[512,1024]{1,0:T(8,128)(2,1)} %get-tuple-element.63), channel_id=1, source_target_pairs={{0,193},{1,64},{64,129},{65,0},{128,65},{129,192},{192,1},{193,128... | collective-permute-start | bytes 3145736 | tf_op jit(solution)/shard_map/ppermute | solution.py:44
  24.4 12.4 %collective-permute-start.6 = (bf16[2176,128]{1,0:T(8,128)(2,1)S(1)}, bf16[2176,128]{1,0:T(8,128)(2,1)S(1)}, u32[]{:S(2)}, u32[]{:S(2)}) collective-permute-start(bf16[2176,128]{1,0:T(8,128)(2,1)S(1)} %collective-permute-done.4.refs_7_), channel_id=1, source_target_pairs={{0,1},{1,0},{2,3},{3,2},{4,5},{5,4},{6,7},{7,6},{8,9},{9,8},{10,11... | collective-permute-start | bytes 1671176 | tf_op jit(solution)/shard_map/ppermute | solution.py:30
  24.4 12.4 %collective-permute-start.7 = (bf16[2176,128]{1,0:T(8,128)(2,1)S(1)}, bf16[2176,128]{1,0:T(8,128)(2,1)S(1)}, u32[]{:S(2)}, u32[]{:S(2)}) collective-permute-start(bf16[2176,128]{1,0:T(8,128)(2,1)S(1)} %collective-permute-done.5.refs_8_), channel_id=1, source_target_pairs={{0,1},{1,0},{2,3},{3,2},{4,5},{5,4},{6,7},{7,6},{8,9},{9,8},{10,11... | collective-permute-start | bytes 1671176 | tf_op jit(solution)/shard_map/ppermute | solution.py:30
  43.8 12.5 %collective-permute-start.10 = (bf16[528,128]{1,0:T(8,128)(2,1)S(1)}, bf16[528,128]{1,0:T(8,128)(2,1)S(1)}, u32[]{:S(2)}, u32[]{:S(2)}) collective-permute-start(bf16[528,128]{1,0:T(8,128)(2,1)S(1)} %get-tuple-element.60), channel_id=1, source_target_pairs={{0,192},{64,0},{128,64},{192,128},{1,193},{65,1},{129,65},{193,129... | collective-permute-start | bytes 405512 | tf_op jit(solution)/shard_map/ppermute | solution.py:30
  49.6 6.7 %collective-permute-start.11 = (bf16[528,128]{1,0:T(8,128)(2,1)S(1)}, bf16[528,128]{1,0:T(8,128)(2,1)S(1)}, u32[]{:S(2)}, u32[]{:S(2)}) collective-permute-start(bf16[528,128]{1,0:T(8,128)(2,1)S(1)} %get-tuple-element.61), channel_id=1, source_target_pairs={{0,64},{64,128},{128,192},{192,0},{1,65},{65,129},{129,193},{193,1... | collective-permute-start | bytes 405512 | tf_op jit(solution)/shard_map/ppermute | solution.py:30
  52.6 8.2 %collective-permute-start.12 = (bf16[528,128]{1,0:T(8,128)(2,1)S(1)}, bf16[528,128]{1,0:T(8,128)(2,1)S(1)}, u32[]{:S(2)}, u32[]{:S(2)}) collective-permute-start(bf16[528,128]{1,0:T(8,128)(2,1)S(1)} %get-tuple-element.62), channel_id=1, source_target_pairs={{0,128},{64,192},{128,0},{192,64},{1,129},{65,193},{129,1},{193,65... | collective-permute-start | bytes 405512 | tf_op jit(solution)/shard_map/ppermute | solution.py:30
  61.0 7.1 %collective-permute-start.15 = (bf16[128,512]{1,0:T(8,128)(2,1)S(1)}, bf16[128,512]{1,0:T(8,128)(2,1)S(1)}, u32[]{:S(2)}, u32[]{:S(2)}) collective-permute-start(bf16[128,512]{1,0:T(8,128)(2,1)S(1)} %merge.1), channel_id=1, source_target_pairs={{0,128},{64,192},{128,0},{192,64},{1,129},{65,193},{129,1},{193,65... | collective-permute-start | bytes 393224 | tf_op jit(solution)/shard_map/ppermute | solution.py:30
  62.4 21.7 %collective-permute-start.19 = (bf16[512,1024]{1,0:T(8,128)(2,1)S(1)}, bf16[512,1024]{1,0:T(8,128)(2,1)S(1)}, u32[]{:S(2)}, u32[]{:S(2)}) collective-permute-start(bf16[512,1024]{1,0:T(8,128)(2,1)S(1)} %copy-done.4), channel_id=1, source_target_pairs={{0,1},{1,0},{2,3},{3,2},{4,5},{5,4},{6,7},{7,6},{8,9},{9,8},{10,11... | collective-permute-start | bytes 3145736 | tf_op jit(solution)/shard_map/ppermute | solution.py:30
  63.8 6.6 %collective-permute-start.16 = (bf16[128,512]{1,0:T(8,128)(2,1)S(1)}, bf16[128,512]{1,0:T(8,128)(2,1)S(1)}, u32[]{:S(2)}, u32[]{:S(2)}) collective-permute-start(bf16[128,512]{1,0:T(8,128)(2,1)S(1)} %merge.1), channel_id=1, source_target_pairs={{0,32},{2,34},{32,0},{34,2},{1,33},{3,35},{33,1},{35,3},{4,36},{6,... | collective-permute-start | bytes 393224 | tf_op jit(solution)/shard_map/ppermute | solution.py:30
  64.3 10.1 %collective-permute-start.17 = (bf16[128,512]{1,0:T(8,128)(2,1)S(1)}, bf16[128,512]{1,0:T(8,128)(2,1)S(1)}, u32[]{:S(2)}, u32[]{:S(2)}) collective-permute-start(bf16[128,512]{1,0:T(8,128)(2,1)S(1)} %merge.1), channel_id=1, source_target_pairs={{0,160},{32,128},{128,32},{160,0},{1,161},{33,129},{129,33},{161,1... | collective-permute-start | bytes 393224 | tf_op jit(solution)/shard_map/ppermute | solution.py:546
  78.4 10.2 %collective-permute-start.32 = (bf16[32,1024]{1,0:T(8,128)(2,1)S(1)}, bf16[32,1024]{1,0:T(8,128)(2,1)S(1)}, u32[]{:S(2)}, u32[]{:S(2)}) collective-permute-start(bf16[32,1024]{1,0:T(8,128)(2,1)S(1)} %get-tuple-element.84), channel_id=1, source_target_pairs={{0,28},{4,0},{8,4},{12,8},{16,12},{20,16},{24,20},{28,24},{1,29},{... | collective-permute-start | bytes 196616 | tf_op jit(solution)/shard_map/ppermute | solution.py:30
  84.0 7.3 %collective-permute-start.28 = (bf16[32,1024]{1,0:T(8,128)(2,1)S(1)}, bf16[32,1024]{1,0:T(8,128)(2,1)S(1)}, u32[]{:S(2)}, u32[]{:S(2)}) collective-permute-start(bf16[32,1024]{1,0:T(8,128)(2,1)S(1)} %get-tuple-element.80), channel_id=1, source_target_pairs={{0,4},{4,8},{8,12},{12,16},{16,20},{20,24},{24,28},{28,0},{1,5},{5... | collective-permute-start | bytes 196616 | tf_op jit(solution)/shard_map/ppermute | solution.py:30
  85.6 5.9 %collective-permute-start.24 = (bf16[32,1024]{1,0:T(8,128)(2,1)S(1)}, bf16[32,1024]{1,0:T(8,128)(2,1)S(1)}, u32[]{:S(2)}, u32[]{:S(2)}) collective-permute-start(bf16[32,1024]{1,0:T(8,128)(2,1)S(1)} %get-tuple-element.73), channel_id=1, source_target_pairs={{0,28},{4,0},{8,4},{12,8},{16,12},{20,16},{24,20},{28,24},{1,29},{... | collective-permute-start | bytes 196616 | tf_op jit(solution)/shard_map/ppermute | solution.py:30
  88.6 5.8 %collective-permute-start.33 = (bf16[64,1024]{1,0:T(8,128)(2,1)S(1)}, bf16[64,1024]{1,0:T(8,128)(2,1)S(1)}, u32[]{:S(2)}, u32[]{:S(2)}) collective-permute-start(bf16[64,1024]{1,0:T(8,128)(2,1)S(1)} %pad_maximum_fusion.3), channel_id=1, source_target_pairs={{0,28},{4,0},{8,4},{12,8},{16,12},{20,16},{24,20},{28,24},{1,29},{... | collective-permute-start | bytes 393224 | tf_op jit(solution)/shard_map/ppermute | solution.py:30
  91.4 5.8 %collective-permute-start.29 = (bf16[64,1024]{1,0:T(8,128)(2,1)S(1)}, bf16[64,1024]{1,0:T(8,128)(2,1)S(1)}, u32[]{:S(2)}, u32[]{:S(2)}) collective-permute-start(bf16[64,1024]{1,0:T(8,128)(2,1)S(1)} %pad_maximum_fusion.2), channel_id=1, source_target_pairs={{0,4},{4,8},{8,12},{12,16},{16,20},{20,24},{24,28},{28,0},{1,5},{5... | collective-permute-start | bytes 393224 | tf_op jit(solution)/shard_map/ppermute | solution.py:30
  91.5 5.8 %collective-permute-start.25 = (bf16[64,1024]{1,0:T(8,128)(2,1)S(1)}, bf16[64,1024]{1,0:T(8,128)(2,1)S(1)}, u32[]{:S(2)}, u32[]{:S(2)}) collective-permute-start(bf16[64,1024]{1,0:T(8,128)(2,1)S(1)} %pad_maximum_fusion.1), channel_id=1, source_target_pairs={{0,28},{4,0},{8,4},{12,8},{16,12},{20,16},{24,20},{28,24},{1,29},{... | collective-permute-start | bytes 393224 | tf_op jit(solution)/shard_map/ppermute | solution.py:30
  94.3 5.8 %collective-permute-start.21 = (bf16[64,1024]{1,0:T(8,128)(2,1)S(1)}, bf16[64,1024]{1,0:T(8,128)(2,1)S(1)}, u32[]{:S(2)}, u32[]{:S(2)}) collective-permute-start(bf16[64,1024]{1,0:T(8,128)(2,1)S(1)} %pad_maximum_fusion), channel_id=1, source_target_pairs={{0,4},{4,8},{8,12},{12,16},{16,20},{20,24},{24,28},{28,0},{1,5},{5... | collective-permute-start | bytes 393224 | tf_op jit(solution)/shard_map/ppermute | solution.py:30
  94.4 5.8 %collective-permute-start.34 = (bf16[64,1024]{1,0:T(8,128)(2,1)S(1)}, bf16[64,1024]{1,0:T(8,128)(2,1)S(1)}, u32[]{:S(2)}, u32[]{:S(2)}) collective-permute-start(bf16[64,1024]{1,0:T(8,128)(2,1)S(1)} %add_convert_fusion.1), channel_id=1, source_target_pairs={{0,28},{4,0},{8,4},{12,8},{16,12},{20,16},{24,20},{28,24},{1,29},{... | collective-permute-start | bytes 393224 | tf_op jit(solution)/shard_map/ppermute | solution.py:30
  97.2 6.6 %collective-permute-start.30 = (bf16[64,1024]{1,0:T(8,128)(2,1)S(1)}, bf16[64,1024]{1,0:T(8,128)(2,1)S(1)}, u32[]{:S(2)}, u32[]{:S(2)}) collective-permute-start(bf16[64,1024]{1,0:T(8,128)(2,1)S(1)} %add_convert_fusion.3), channel_id=1, source_target_pairs={{0,4},{4,8},{8,12},{12,16},{16,20},{20,24},{24,28},{28,0},{1,5},{5... | collective-permute-start | bytes 393224 | tf_op jit(solution)/shard_map/ppermute | solution.py:30
  97.4 6.5 %collective-permute-start.26 = (bf16[64,1024]{1,0:T(8,128)(2,1)S(1)}, bf16[64,1024]{1,0:T(8,128)(2,1)S(1)}, u32[]{:S(2)}, u32[]{:S(2)}) collective-permute-start(bf16[64,1024]{1,0:T(8,128)(2,1)S(1)} %add_convert_fusion.5), channel_id=1, source_target_pairs={{0,28},{4,0},{8,4},{12,8},{16,12},{20,16},{24,20},{28,24},{1,29},{... | collective-permute-start | bytes 393224 | tf_op jit(solution)/shard_map/ppermute | solution.py:30
  100.2 6.6 %collective-permute-start.22 = (bf16[64,1024]{1,0:T(8,128)(2,1)S(1)}, bf16[64,1024]{1,0:T(8,128)(2,1)S(1)}, u32[]{:S(2)}, u32[]{:S(2)}) collective-permute-start(bf16[64,1024]{1,0:T(8,128)(2,1)S(1)} %add_convert_fusion.7), channel_id=1, source_target_pairs={{0,4},{4,8},{8,12},{12,16},{16,20},{20,24},{24,28},{28,0},{1,5},{5... | collective-permute-start | bytes 393224 | tf_op jit(solution)/shard_map/ppermute | solution.py:30
  100.3 6.6 %collective-permute-start.35 = (bf16[64,1024]{1,0:T(8,128)(2,1)S(1)}, bf16[64,1024]{1,0:T(8,128)(2,1)S(1)}, u32[]{:S(2)}, u32[]{:S(2)}) collective-permute-start(bf16[64,1024]{1,0:T(8,128)(2,1)S(1)} %add_convert_fusion), channel_id=1, source_target_pairs={{0,28},{4,0},{8,4},{12,8},{16,12},{20,16},{24,20},{28,24},{1,29},{... | collective-permute-start | bytes 393224 | tf_op jit(solution)/shard_map/ppermute | solution.py:30
  103.8 6.0 %collective-permute-start.31 = (bf16[64,1024]{1,0:T(8,128)(2,1)S(1)}, bf16[64,1024]{1,0:T(8,128)(2,1)S(1)}, u32[]{:S(2)}, u32[]{:S(2)}) collective-permute-start(bf16[64,1024]{1,0:T(8,128)(2,1)S(1)} %add_convert_fusion.2), channel_id=1, source_target_pairs={{0,4},{4,8},{8,12},{12,16},{16,20},{20,24},{24,28},{28,0},{1,5},{5... | collective-permute-start | bytes 393224 | tf_op jit(solution)/shard_map/ppermute | solution.py:30
  104.0 5.8 %collective-permute-start.27 = (bf16[64,1024]{1,0:T(8,128)(2,1)S(1)}, bf16[64,1024]{1,0:T(8,128)(2,1)S(1)}, u32[]{:S(2)}, u32[]{:S(2)}) collective-permute-start(bf16[64,1024]{1,0:T(8,128)(2,1)S(1)} %add_convert_fusion.4), channel_id=1, source_target_pairs={{0,28},{4,0},{8,4},{12,8},{16,12},{20,16},{24,20},{28,24},{1,29},{... | collective-permute-start | bytes 393224 | tf_op jit(solution)/shard_map/ppermute | solution.py:30
  (9 other events, 120.6 us)

commit v2 on v1

--- a/solution.py
+++ b/solution.py
@@ -376,12 +376,14 @@
 
 def project_body(*refs):
     x_own, x_other = refs[0:2]
-    weights = refs[2:4]
-    out = refs[4:13]
-    x_ref, w_ref, sems = refs[13:16]
+    weights = refs[2:6]
+    out = refs[6:15]
+    x_ref, w_ref, sems = refs[15:18]
     depth = weights[0].shape[0]
     copies = [
-        pltpu.make_async_copy(weight, w_ref.at[pl.ds(i * depth, depth)], sems.at[i])
+        pltpu.make_async_copy(
+            weight, w_ref.at[i // 2, pl.ds((i % 2) * depth, depth)], sems.at[i]
+        )
         for i, weight in enumerate(weights)
     ]
     for copy in copies:
@@ -389,38 +391,40 @@
     z = lax.axis_index("z")
     for r in range(8):
         part = pl.multiple_of(lax.rem(z + r, 8) * 16, 16)
-        for j in range(4):
-            row = r * 64 + j * 16
+        for j in range(2):
+            row = r * 32 + j * 16
             source = pl.ds(pl.multiple_of(part + j * TOK, 16), 16)
             x_ref[row : row + 16, 0:depth] = x_own[source, :]
             x_ref[row : row + 16, depth : 2 * depth] = x_other[source, :]
-    for copy in copies:
-        copy.wait()
-    for n in range(4):
-        cols = slice(n * 256, (n + 1) * 256)
-        y = jnp.dot(x_ref[...], w_ref[:, cols], preferred_element_type=F32).astype(BF16)
-        for r in range(8):
-            if r < 4:
-                out[r][:, cols] = y[r * 64 : (r + 1) * 64]
-            elif r == 4:
-                out[4][:, cols] = y[256:288]
-                out[5][:, cols] = y[288:320]
-            else:
-                out[r + 1][:, cols] = y[r * 64 : (r + 1) * 64]
+    for side in range(2):
+        for copy in copies[side * 2 : side * 2 + 2]:
+            copy.wait()
+        for n in range(4):
+            cols = slice(n * 256, (n + 1) * 256)
+            y = jnp.dot(x_ref[...], w_ref[side, :, cols], preferred_element_type=F32).astype(BF16)
+            cols = slice(side * WIDE + n * 256, side * WIDE + (n + 1) * 256)
+            for r in range(8):
+                if r < 4:
+                    out[r][:, cols] = y[r * 32 : (r + 1) * 32]
+                elif r == 4:
+                    out[4][:, cols] = y[128:144]
+                    out[5][:, cols] = y[144:160]
+                else:
+                    out[r + 1][:, cols] = y[r * 32 : (r + 1) * 32]
 
 
 def project(x_own, x_other, weights):
-    full = jax.ShapeDtypeStruct((64, WIDE), BF16)
-    half = jax.ShapeDtypeStruct((32, WIDE), BF16)
+    full = jax.ShapeDtypeStruct((32, 2 * WIDE), BF16)
+    half = jax.ShapeDtypeStruct((16, 2 * WIDE), BF16)
     return pl.pallas_call(
         project_body,
         out_shape=[full] * 4 + [half] * 2 + [full] * 3,
-        in_specs=[VMEM] * 2 + [HBM] * 2,
+        in_specs=[VMEM] * 2 + [HBM] * 4,
         out_specs=[VMEM] * 9,
         scratch_shapes=[
-            pltpu.VMEM((512, 1024), BF16),
-            pltpu.VMEM((1024, WIDE), BF16),
-            pltpu.SemaphoreType.DMA((2,)),
+            pltpu.VMEM((256, 1024), BF16),
+            pltpu.VMEM((2, 1024, WIDE), BF16),
+            pltpu.SemaphoreType.DMA((4,)),
         ],
         compiler_params=params(12),
         name="project",
@@ -448,14 +452,17 @@
 def order_body(*refs):
     out_ref = refs[6]
     yp, yl, xh = (lax.axis_index(name) for name in ("yp", "yl", "xh"))
-    for side in range(2):
-        kept, up, down = refs[side * 3 : side * 3 + 3]
+    for pair in range(2):
+        kept, up, down = refs[pair * 3 : pair * 3 + 3]
         total = kept[...].astype(F32) + up[...].astype(F32) + down[...].astype(F32)
         total = total.astype(BF16)
-        column = pl.ds(pl.multiple_of((yl if side == 0 else 1 - yl) * WIDE, WIDE), WIDE)
-        for j in range(4):
-            place = (yp if j % 2 == 0 else 1 - yp) * 2 + (xh if j < 2 else 1 - xh)
-            out_ref[place, :, column] = total[j * 16 : (j + 1) * 16]
+        for side in range(2):
+            column = pl.ds(pl.multiple_of((yl if side == 0 else 1 - yl) * WIDE, WIDE), WIDE)
+            for j in range(2):
+                place = (yp if j == 0 else 1 - yp) * 2 + (xh if pair == 0 else 1 - xh)
+                out_ref[place, :, column] = total[
+                    j * 16 : (j + 1) * 16, side * WIDE : (side + 1) * WIDE
+                ]
 
 
 def ordered(sums):
@@ -541,14 +548,15 @@
     attended, w_kept_pair, w_other_pair = lax.optimization_barrier(
         (attended, w_kept_pair, w_other_pair)
     )
-    w_other = to_other_core(w_away)
-
+
+    w_other = to_other_core(after(w_away, attended))
+    weights = (w_kept, w_other, w_kept_pair, w_other_pair)
+    below, beside = along_y(attended, 2), along_x(attended, 2)
     corner = lax.ppermute(attended, ("yp", "xh"), [(i, 3 - i) for i in range(4)])
-    blocks = (attended, along_y(attended, 2), along_x(attended, 2), corner)
-    x_own = jnp.concatenate(blocks, axis=0)
-    x_other = to_other_core(x_own)
-    near = project(x_own, x_other, (w_kept, w_other))
-    pair = project(x_own, x_other, (w_kept_pair, w_other_pair))
+    near = jnp.concatenate([attended, below], axis=0)
+    pair = jnp.concatenate([beside, corner], axis=0)
+    near = project(near, to_other_core(near), weights)
+    pair = project(pair, to_other_core(pair), weights)
     blocks = ordered((*sum_over_z(near), *sum_over_z(pair))).reshape(64, 2 * WIDE)
     spread = lax.all_to_all(blocks, ("yp", "xh", "xl", "core"), 0, 0, tiled=True)
     return finish(spread)

time: 132 us -> 130 us (0.985)
  waiting for transfers between devices: 30.9 us -> 27.4 us
  Pallas kernels: 19.6 us -> 22.6 us
  starting transfers between devices: 61.7 us -> 60 us
    pallas_call x2, Pallas kernels: 10 us -> 12.4 us  [attend(): pl.pallas_call(lambda *refs: attend_body(first, last, sources, *refs), ou...]
    ppermute x33 -> x34, waiting for transfers between devices: 26.9 us -> 24.8 us  [moved(): lax.ppermute(value, axis, [(i, (i + step) % size) for i in range(size)])]
    ppermute x1, waiting for transfers between devices: 4.01 us -> 2.6 us  [shards(): lax.ppermute(attended, ('yp', 'xh'), [(i, 3 - i) for i in range(4)])]
    ppermute x33 -> x34, starting transfers between devices: 53.9 us -> 53.6 us  [moved(): lax.ppermute(value, axis, [(i, (i + step) % size) for i in range(size)])]
  transfers between devices with their start and end apart: 36 -> 37, of which waited for: 12 -> 13; matrix products, arithmetic and copies ran while one was open for 0% -> 0% of each run, Pallas kernels for 12% -> 15%
where the time goes in v2:
time: 130 us
  starting transfers between devices  60 us (46%)
  waiting for transfers between devices  27.4 us (21%)
  Pallas kernels  22.6 us (17%)
  blocking collectives  18.5 us (14%)
    ppermute x34, starting transfers between devices, moved(): lax.ppermute(value, axis, [(i, (i + step) % size) for i in range(size)])  53.6 us
    ppermute x34, waiting for transfers between devices, moved(): lax.ppermute(value, axis, [(i, (i + step) % size) for i in range(size)])  24.8 us
    all_to_all x1, blocking collectives, shards(): lax.all_to_all(blocks, ('yp', 'xh', 'xl', 'core'), 0, 0, tiled=True)  18.5 us
    pallas_call x2, Pallas kernels, attend(): pl.pallas_call(lambda *refs: attend_body(first, last, sources, *refs), ou...  12.4 us
    ppermute x2, starting transfers between devices, to_y_pair(): return lax.ppermute(value, ('yp', 'yl', 'core'), pairs)  4.01 us
    pallas_call x2, Pallas kernels, project(): pl.pallas_call(project_body, out_shape=[full] * 4 + [half] * 2 + [full] *...  3.6 us
    pallas_call x1, Pallas kernels, halves(): pl.pallas_call(halves_body, out_shape=[jax.ShapeDtypeStruct((weight.shape...  2.9 us
    pallas_call x1, Pallas kernels, pack(): pl.pallas_call(pack_body, out_shape=[jax.ShapeDtypeStruct((TOK + 16, HEAD...  2.67 us
  transfers between devices with their start and end apart: 37, of which 13 were waited for; matrix products, arithmetic and copies ran while one was open for 0% of the time, Pallas kernels for 15%

profile of v2, /device:TPU:1, one launch (start us, length us, event | category | flops | bytes accessed | tf_op | source)
XLA Modules:
  0.0 129.6 jit_solution(13466625513405065847)
XLA Ops:
  0.0 2.7 %pack.1 = (bf16[144,512]{1,0:T(8,128)(2,1)}, bf16[2176,128]{1,0:T(8,128)(2,1)}) custom-call(bf16[128,512]{1,0:T(8,128)(2,1)} %q_hbm.1, bf16[1024,128]{1,0:T(8,128)(2,1)} %bitcast.3, bf16[1024,128]{1,0:T(8,128)(2,1)} %bitcast.4, bf16[128,1024]{1,0:T(8,128)(2,1)} %nk_hbm.1, bf16[128,1024]{1,0:T(8,128)(2,1)} %nv_hbm.1, s32[1,128]{1,0:T(1,128)} %bitcast.5), custom_call_target="tpu_custom_call" | custom-call | tf_op jit(solution)/shard_map/pack/pallas_call | solution.py:107
  2.7 2.1 %collective-permute-start.4 = (bf16[2176,128]{1,0:T(8,128)(2,1)}, bf16[2176,128]{1,0:T(8,128)(2,1)S(1)}, u32[]{:S(2)}, u32[]{:S(2)}) collective-permute-start(bf16[2176,128]{1,0:T(8,128)(2,1)} %get-tuple-element.58.refs_5_), channel_id=1, source_target_pairs={{0,2},{2,32},{32,34},{34,0},{1,3},{3,33},{33,35},{35,1},{4,6},{6,3... | collective-permute-start | bytes 1671176 | tf_op jit(solution)/shard_map/ppermute | solution.py:30
  7.6 1.4 %collective-permute-start.1 = (bf16[144,512]{1,0:T(8,128)(2,1)}, bf16[144,512]{1,0:T(8,128)(2,1)S(1)}, u32[]{:S(2)}, u32[]{:S(2)}) collective-permute-start(bf16[144,512]{1,0:T(8,128)(2,1)} %get-tuple-element.46.refs_1_), channel_id=1, source_target_pairs={{0,192},{64,0},{128,64},{192,128},{1,193},{65,1},{129,65},{193,129... | collective-permute-start | bytes 442376 | tf_op jit(solution)/shard_map/ppermute | solution.py:30
  9.0 1.6 %collective-permute-start.2 = (bf16[144,512]{1,0:T(8,128)(2,1)}, bf16[144,512]{1,0:T(8,128)(2,1)S(1)}, u32[]{:S(2)}, u32[]{:S(2)}) collective-permute-start(bf16[144,512]{1,0:T(8,128)(2,1)} %get-tuple-element.46.refs_1_), channel_id=1, source_target_pairs={{0,128},{64,192},{128,0},{192,64},{1,129},{65,193},{129,1},{193,65... | collective-permute-start | bytes 442376 | tf_op jit(solution)/shard_map/ppermute | solution.py:30
  12.1 2.9 %halves.1 = (bf16[512,1024]{1,0:T(8,128)(2,1)}, bf16[512,1024]{1,0:T(8,128)(2,1)}) custom-call(bf16[512,2048]{1,0:T(8,128)(2,1)} %w_hbm), custom_call_target="tpu_custom_call" | custom-call | tf_op jit(solution)/shard_map/halves/pallas_call | solution.py:135
  16.3 3.9 %collective-permute-start.3 = (bf16[2176,128]{1,0:T(8,128)(2,1)S(1)}, bf16[2176,128]{1,0:T(8,128)(2,1)S(1)}, u32[]{:S(2)}, u32[]{:S(2)}) collective-permute-start(bf16[2176,128]{1,0:T(8,128)(2,1)S(1)} %copy-done.1), channel_id=1, source_target_pairs={{0,1},{1,0},{2,3},{3,2},{4,5},{5,4},{6,7},{7,6},{8,9},{9,8},{10,11... | collective-permute-start | bytes 1671176 | tf_op jit(solution)/shard_map/ppermute | solution.py:30
  20.4 3.0 %collective-permute-start.13 = (bf16[512,1024]{1,0:T(8,128)(2,1)}, bf16[512,1024]{1,0:T(8,128)(2,1)S(1)}, u32[]{:S(2)}, u32[]{:S(2)}) collective-permute-start(bf16[512,1024]{1,0:T(8,128)(2,1)} %get-tuple-element.50.refs_2_), channel_id=1, source_target_pairs={{0,64},{1,193},{64,0},{65,129},{128,192},{129,65},{192,128},{193,1... | collective-permute-start | bytes 3145736 | tf_op jit(solution)/shard_map/ppermute | solution.py:44
  25.0 4.6 %attend.2 = (bf16[256,2048]{1,0:T(8,128)(2,1)S(1)}, f32[1,512]{1,0:T(1,128)S(1)}, f32[1,2048]{1,0:T(1,128)S(1)}, f32[144,2048]{1,0:T(8,128)S(1)}, bf16[512,128]{1,0:T(8,128)(2,1)S(1)}) custom-call(s32[8]{0:T(128)S(1)} %copy-done.3, bf16[144,512]{1,0:T(8,128)(2,1)S(1)} %copy-done.2, bf16[144,512]{1,0:T(8,128)(2,1)S(1)} %collective-permute-done.refs_2_, ...), custom_call_target="tpu_custom_call" | custom-call | flops 1000000 | bytes 1024 | tf_op jit(solution)/shard_map/attend/pallas_call | solution.py:332
  29.6 6.4 %collective-permute-done.8.refs_8_ = bf16[2176,128]{1,0:T(8,128)(2,1)S(1)} collective-permute-done((bf16[2176,128]{1,0:T(8,128)(2,1)S(1)}, bf16[2176,128]{1,0:T(8,128)(2,1)S(1)}, u32[]{:S(2)}, u32[]{:S(2)}) %collective-permute-start.8) | collective-permute-done | bytes 557088 | tf_op jit(solution)/shard_map/ppermute | solution.py:30
  36.8 1.6 %collective-permute-done.9.refs_9_ = bf16[2176,128]{1,0:T(8,128)(2,1)S(1)} collective-permute-done((bf16[2176,128]{1,0:T(8,128)(2,1)S(1)}, bf16[2176,128]{1,0:T(8,128)(2,1)S(1)}, u32[]{:S(2)}, u32[]{:S(2)}) %collective-permute-start.9) | collective-permute-done | bytes 557088 | tf_op jit(solution)/shard_map/ppermute | solution.py:30
  38.4 7.8 %attend.3 = (bf16[528,128]{1,0:T(8,128)(2,1)S(1)}, bf16[528,128]{1,0:T(8,128)(2,1)S(1)}, bf16[528,128]{1,0:T(8,128)(2,1)S(1)}, bf16[528,128]{1,0:T(8,128)(2,1)S(1)}) custom-call(s32[8]{0:T(128)S(1)} %copy-done.3, bf16[256,2048]{1,0:T(8,128)(2,1)S(1)} %get-tuple-element.53.refs_1_, f32[1,512]{1,0:T(1,128)S(1)} %get-tuple-element.54.refs_2_, ...), custom_call_target="tpu_custom_call" | custom-call | flops 1000000 | bytes 1024 | tf_op jit(solution)/shard_map/attend/pallas_call | solution.py:332
  46.2 7.4 %collective-permute-start.10 = (bf16[528,128]{1,0:T(8,128)(2,1)S(1)}, bf16[528,128]{1,0:T(8,128)(2,1)S(1)}, u32[]{:S(2)}, u32[]{:S(2)}) collective-permute-start(bf16[528,128]{1,0:T(8,128)(2,1)S(1)} %get-tuple-element.61), channel_id=1, source_target_pairs={{0,192},{64,0},{128,64},{192,128},{1,193},{65,1},{129,65},{193,129... | collective-permute-start | bytes 405512 | tf_op jit(solution)/shard_map/ppermute | solution.py:30
  54.8 1.8 %collective-permute-done.10.refs_1_ = bf16[528,128]{1,0:T(8,128)(2,1)S(1)} collective-permute-done((bf16[528,128]{1,0:T(8,128)(2,1)S(1)}, bf16[528,128]{1,0:T(8,128)(2,1)S(1)}, u32[]{:S(2)}, u32[]{:S(2)}) %collective-permute-start.10) | collective-permute-done | bytes 135200 | tf_op jit(solution)/shard_map/ppermute | solution.py:30
  56.6 3.5 %collective-permute-done.11.refs_2_ = bf16[528,128]{1,0:T(8,128)(2,1)S(1)} collective-permute-done((bf16[528,128]{1,0:T(8,128)(2,1)S(1)}, bf16[528,128]{1,0:T(8,128)(2,1)S(1)}, u32[]{:S(2)}, u32[]{:S(2)}) %collective-permute-start.11) | collective-permute-done | bytes 135200 | tf_op jit(solution)/shard_map/ppermute | solution.py:30
  61.1 2.4 %collective-permute-start.27 = (bf16[128,512]{1,0:T(8,128)(2,1)S(1)}, bf16[128,512]{1,0:T(8,128)(2,1)S(1)}, u32[]{:S(2)}, u32[]{:S(2)}) collective-permute-start(bf16[128,512]{1,0:T(8,128)(2,1)S(1)} %merge.1), channel_id=1, source_target_pairs={{0,160},{32,128},{128,32},{160,0},{1,161},{33,129},{129,33},{161,1... | collective-permute-start | bytes 393224 | tf_op jit(solution)/shard_map/ppermute | solution.py:555
  63.5 2.8 %collective-permute-start.15 = (bf16[128,512]{1,0:T(8,128)(2,1)S(1)}, bf16[128,512]{1,0:T(8,128)(2,1)S(1)}, u32[]{:S(2)}, u32[]{:S(2)}) collective-permute-start(bf16[128,512]{1,0:T(8,128)(2,1)S(1)} %merge.1), channel_id=1, source_target_pairs={{0,128},{64,192},{128,0},{192,64},{1,129},{65,193},{129,1},{193,65... | collective-permute-start | bytes 393224 | tf_op jit(solution)/shard_map/ppermute | solution.py:30
  66.7 2.6 %collective-permute-done.27 = bf16[128,512]{1,0:T(8,128)(2,1)S(1)} collective-permute-done((bf16[128,512]{1,0:T(8,128)(2,1)S(1)}, bf16[128,512]{1,0:T(8,128)(2,1)S(1)}, u32[]{:S(2)}, u32[]{:S(2)}) %collective-permute-start.27) | collective-permute-done | bytes 131104 | tf_op jit(solution)/shard_map/ppermute | solution.py:555
  69.3 1.7 %collective-permute-start.28 = (bf16[256,512]{1,0:T(8,128)(2,1)S(1)}, bf16[256,512]{1,0:T(8,128)(2,1)S(1)}, u32[]{:S(2)}, u32[]{:S(2)}) collective-permute-start(bf16[256,512]{1,0:T(8,128)(2,1)S(1)} %constant_dynamic-update-slice_fusion.2.refs_0_), channel_id=1, source_target_pairs={{0,1},{1,0},{2,3},{3,2},{4,5},{5,4},{6,7},{7,6},{8,9},{9,8},{10,11... | collective-permute-start | bytes 786440 | tf_op jit(solution)/shard_map/ppermute | solution.py:30
  71.1 2.1 %collective-permute-done.15 = bf16[128,512]{1,0:T(8,128)(2,1)S(1)} collective-permute-done((bf16[128,512]{1,0:T(8,128)(2,1)S(1)}, bf16[128,512]{1,0:T(8,128)(2,1)S(1)}, u32[]{:S(2)}, u32[]{:S(2)}) %collective-permute-start.15) | collective-permute-done | bytes 131104 | tf_op jit(solution)/shard_map/ppermute | solution.py:30
  73.8 1.8 %project.3 = (bf16[32,2048]{1,0:T(8,128)(2,1)S(1)}, bf16[32,2048]{1,0:T(8,128)(2,1)S(1)}, bf16[32,2048]{1,0:T(8,128)(2,1)S(1)}, bf16[32,2048]{1,0:T(8,128)(2,1)S...) custom-call(bf16[256,512]{1,0:T(8,128)(2,1)S(1)} %constant_dynamic-u, ...), custom_call_target="tpu_custom_call" | custom-call | tf_op jit(solution)/shard_map/project/pallas_call | solution.py:419
  75.6 5.6 %collective-permute-start.33 = (bf16[16,2048]{1,0:T(8,128)(2,1)S(1)}, bf16[16,2048]{1,0:T(8,128)(2,1)S(1)}, u32[]{:S(2)}, u32[]{:S(2)}) collective-permute-start(bf16[16,2048]{1,0:T(8,128)(2,1)S(1)} %get-tuple-element.86), channel_id=1, source_target_pairs={{0,28},{4,0},{8,4},{12,8},{16,12},{20,16},{24,20},{28,24},{1,29},{... | collective-permute-start | bytes 196616 | tf_op jit(solution)/shard_map/ppermute | solution.py:30
  81.3 1.8 %project.2 = (bf16[32,2048]{1,0:T(8,128)(2,1)S(1)}, bf16[32,2048]{1,0:T(8,128)(2,1)S(1)}, bf16[32,2048]{1,0:T(8,128)(2,1)S(1)}, bf16[32,2048]{1,0:T(8,128)(2,1)S...) custom-call(bf16[256,512]{1,0:T(8,128)(2,1)S(1)} %constant_dynamic-u, ...), custom_call_target="tpu_custom_call" | custom-call | tf_op jit(solution)/shard_map/project/pallas_call | solution.py:419
  83.1 2.7 %collective-permute-start.22 = (bf16[16,2048]{1,0:T(8,128)(2,1)S(1)}, bf16[16,2048]{1,0:T(8,128)(2,1)S(1)}, u32[]{:S(2)}, u32[]{:S(2)}) collective-permute-start(bf16[16,2048]{1,0:T(8,128)(2,1)S(1)} %get-tuple-element.77), channel_id=1, source_target_pairs={{0,28},{4,0},{8,4},{12,8},{16,12},{20,16},{24,20},{28,24},{1,29},{... | collective-permute-start | bytes 196616 | tf_op jit(solution)/shard_map/ppermute | solution.py:30
  85.9 2.7 %collective-permute-start.34 = (bf16[32,2048]{1,0:T(8,128)(2,1)S(1)}, bf16[32,2048]{1,0:T(8,128)(2,1)S(1)}, u32[]{:S(2)}, u32[]{:S(2)}) collective-permute-start(bf16[32,2048]{1,0:T(8,128)(2,1)S(1)} %pad_maximum_fusion.3), channel_id=1, source_target_pairs={{0,28},{4,0},{8,4},{12,8},{16,12},{20,16},{24,20},{28,24},{1,29},{... | collective-permute-start | bytes 393224 | tf_op jit(solution)/shard_map/ppermute | solution.py:30
  88.8 2.7 %collective-permute-start.23 = (bf16[32,2048]{1,0:T(8,128)(2,1)S(1)}, bf16[32,2048]{1,0:T(8,128)(2,1)S(1)}, u32[]{:S(2)}, u32[]{:S(2)}) collective-permute-start(bf16[32,2048]{1,0:T(8,128)(2,1)S(1)} %pad_maximum_fusion.1), channel_id=1, source_target_pairs={{0,28},{4,0},{8,4},{12,8},{16,12},{20,16},{24,20},{28,24},{1,29},{... | collective-permute-start | bytes 393224 | tf_op jit(solution)/shard_map/ppermute | solution.py:30
  91.8 2.7 %collective-permute-start.35 = (bf16[32,2048]{1,0:T(8,128)(2,1)S(1)}, bf16[32,2048]{1,0:T(8,128)(2,1)S(1)}, u32[]{:S(2)}, u32[]{:S(2)}) collective-permute-start(bf16[32,2048]{1,0:T(8,128)(2,1)S(1)} %add_convert_fusion.1), channel_id=1, source_target_pairs={{0,28},{4,0},{8,4},{12,8},{16,12},{20,16},{24,20},{28,24},{1,29},{... | collective-permute-start | bytes 393224 | tf_op jit(solution)/shard_map/ppermute | solution.py:30
  94.7 2.7 %collective-permute-start.24 = (bf16[32,2048]{1,0:T(8,128)(2,1)S(1)}, bf16[32,2048]{1,0:T(8,128)(2,1)S(1)}, u32[]{:S(2)}, u32[]{:S(2)}) collective-permute-start(bf16[32,2048]{1,0:T(8,128)(2,1)S(1)} %add_convert_fusion.5), channel_id=1, source_target_pairs={{0,28},{4,0},{8,4},{12,8},{16,12},{20,16},{24,20},{28,24},{1,29},{... | collective-permute-start | bytes 393224 | tf_op jit(solution)/shard_map/ppermute | solution.py:30
  97.6 2.7 %collective-permute-start.36 = (bf16[32,2048]{1,0:T(8,128)(2,1)S(1)}, bf16[32,2048]{1,0:T(8,128)(2,1)S(1)}, u32[]{:S(2)}, u32[]{:S(2)}) collective-permute-start(bf16[32,2048]{1,0:T(8,128)(2,1)S(1)} %add_convert_fusion), channel_id=1, source_target_pairs={{0,28},{4,0},{8,4},{12,8},{16,12},{20,16},{24,20},{28,24},{1,29},{... | collective-permute-start | bytes 393224 | tf_op jit(solution)/shard_map/ppermute | solution.py:30
  100.8 3.1 %collective-permute-start.25 = (bf16[32,2048]{1,0:T(8,128)(2,1)S(1)}, bf16[32,2048]{1,0:T(8,128)(2,1)S(1)}, u32[]{:S(2)}, u32[]{:S(2)}) collective-permute-start(bf16[32,2048]{1,0:T(8,128)(2,1)S(1)} %add_convert_fusion.4), channel_id=1, source_target_pairs={{0,28},{4,0},{8,4},{12,8},{16,12},{20,16},{24,20},{28,24},{1,29},{... | collective-permute-start | bytes 393224 | tf_op jit(solution)/shard_map/ppermute | solution.py:30
  104.3 2.4 %collective-permute-done.32.refs_4_ = bf16[32,2048]{1,0:T(8,128)(2,1)S(1)} collective-permute-done((bf16[32,2048]{1,0:T(8,128)(2,1)S(1)}, bf16[32,2048]{1,0:T(8,128)(2,1)S(1)}, u32[]{:S(2)}, u32[]{:S(2)}) %collective-permute-start.32) | collective-permute-done | bytes 131104 | tf_op jit(solution)/shard_map/ppermute | solution.py:30
  106.7 3.3 %collective-permute-done.21.refs_1_ = bf16[32,2048]{1,0:T(8,128)(2,1)S(1)} collective-permute-done((bf16[32,2048]{1,0:T(8,128)(2,1)S(1)}, bf16[32,2048]{1,0:T(8,128)(2,1)S(1)}, u32[]{:S(2)}, u32[]{:S(2)}) %collective-permute-start.21) | collective-permute-done | bytes 131104 | tf_op jit(solution)/shard_map/ppermute | solution.py:30
  110.2 18.5 %all_to_all.11 = bf16[16,4,2048]{2,1,0:T(4,128)(2,1)S(1)} all-to-all(bf16[16,4,2048]{2,1,0:T(4,128)(2,1)S(1)} %all_to_all.7), channel_id=1, replica_groups=mesh['yp'=2,'yl'=2,'xh'=2,'z'=8,'xl'=2,'core'=2] {'yp','xh','xl','core'}, dimensions={0} | all-to-all | bytes 524288 | tf_op jit(solution)/shard_map/all_to_all | solution.py:561
  (88 shorter events, 13.9 us)
Async XLA Ops:
  2.7 17.5 %collective-permute-start.4 = (bf16[2176,128]{1,0:T(8,128)(2,1)}, bf16[2176,128]{1,0:T(8,128)(2,1)S(1)}, u32[]{:S(2)}, u32[]{:S(2)}) collective-permute-start(bf16[2176,128]{1,0:T(8,128)(2,1)} %get-tuple-element.58.refs_5_), channel_id=1, source_target_pairs={{0,2},{2,32},{32,34},{34,0},{1,3},{3,33},{33,35},{35,1},{4,6},{6,3... | collective-permute-start | bytes 1671176 | tf_op jit(solution)/shard_map/ppermute | solution.py:30
  4.8 15.4 %collective-permute-start.5 = (bf16[2176,128]{1,0:T(8,128)(2,1)}, bf16[2176,128]{1,0:T(8,128)(2,1)S(1)}, u32[]{:S(2)}, u32[]{:S(2)}) collective-permute-start(bf16[2176,128]{1,0:T(8,128)(2,1)} %get-tuple-element.58.refs_5_), channel_id=1, source_target_pairs={{0,34},{2,0},{32,2},{34,32},{1,35},{3,1},{33,3},{35,33},{4,38},{6,... | collective-permute-start | bytes 1671176 | tf_op jit(solution)/shard_map/ppermute | solution.py:30
  6.2 5.9 %collective-permute-start = (bf16[144,512]{1,0:T(8,128)(2,1)}, bf16[144,512]{1,0:T(8,128)(2,1)S(1)}, u32[]{:S(2)}, u32[]{:S(2)}) collective-permute-start(bf16[144,512]{1,0:T(8,128)(2,1)} %get-tuple-element.46.refs_1_), channel_id=1, source_target_pairs={{0,64},{64,128},{128,192},{192,0},{1,65},{65,129},{129,193},{193,1... | collective-permute-start | bytes 442376 | tf_op jit(solution)/shard_map/ppermute | solution.py:30
  7.6 7.4 %collective-permute-start.1 = (bf16[144,512]{1,0:T(8,128)(2,1)}, bf16[144,512]{1,0:T(8,128)(2,1)S(1)}, u32[]{:S(2)}, u32[]{:S(2)}) collective-permute-start(bf16[144,512]{1,0:T(8,128)(2,1)} %get-tuple-element.46.refs_1_), channel_id=1, source_target_pairs={{0,192},{64,0},{128,64},{192,128},{1,193},{65,1},{129,65},{193,129... | collective-permute-start | bytes 442376 | tf_op jit(solution)/shard_map/ppermute | solution.py:30
  9.0 7.3 %collective-permute-start.2 = (bf16[144,512]{1,0:T(8,128)(2,1)}, bf16[144,512]{1,0:T(8,128)(2,1)S(1)}, u32[]{:S(2)}, u32[]{:S(2)}) collective-permute-start(bf16[144,512]{1,0:T(8,128)(2,1)} %get-tuple-element.46.refs_1_), channel_id=1, source_target_pairs={{0,128},{64,192},{128,0},{192,64},{1,129},{65,193},{129,1},{193,65... | collective-permute-start | bytes 442376 | tf_op jit(solution)/shard_map/ppermute | solution.py:30
  16.3 8.1 %collective-permute-start.3 = (bf16[2176,128]{1,0:T(8,128)(2,1)S(1)}, bf16[2176,128]{1,0:T(8,128)(2,1)S(1)}, u32[]{:S(2)}, u32[]{:S(2)}) collective-permute-start(bf16[2176,128]{1,0:T(8,128)(2,1)S(1)} %copy-done.1), channel_id=1, source_target_pairs={{0,1},{1,0},{2,3},{3,2},{4,5},{5,4},{6,7},{7,6},{8,9},{9,8},{10,11... | collective-permute-start | bytes 1671176 | tf_op jit(solution)/shard_map/ppermute | solution.py:30
  20.2 15.7 %collective-permute-start.8 = (bf16[2176,128]{1,0:T(8,128)(2,1)S(1)}, bf16[2176,128]{1,0:T(8,128)(2,1)S(1)}, u32[]{:S(2)}, u32[]{:S(2)}) collective-permute-start(bf16[2176,128]{1,0:T(8,128)(2,1)S(1)} %copy-done.1), channel_id=1, source_target_pairs={{0,32},{2,34},{32,0},{34,2},{1,33},{3,35},{33,1},{35,3},{4,36},{6,... | collective-permute-start | bytes 1671176 | tf_op jit(solution)/shard_map/ppermute | solution.py:30
  20.4 39.9 %collective-permute-start.13 = (bf16[512,1024]{1,0:T(8,128)(2,1)}, bf16[512,1024]{1,0:T(8,128)(2,1)S(1)}, u32[]{:S(2)}, u32[]{:S(2)}) collective-permute-start(bf16[512,1024]{1,0:T(8,128)(2,1)} %get-tuple-element.50.refs_2_), channel_id=1, source_target_pairs={{0,64},{1,193},{64,0},{65,129},{128,192},{129,65},{192,128},{193,1... | collective-permute-start | bytes 3145736 | tf_op jit(solution)/shard_map/ppermute | solution.py:44
  23.4 36.9 %collective-permute-start.14 = (bf16[512,1024]{1,0:T(8,128)(2,1)}, bf16[512,1024]{1,0:T(8,128)(2,1)S(1)}, u32[]{:S(2)}, u32[]{:S(2)}) collective-permute-start(bf16[512,1024]{1,0:T(8,128)(2,1)} %get-tuple-element.66), channel_id=1, source_target_pairs={{0,193},{1,64},{64,129},{65,0},{128,65},{129,192},{192,1},{193,128... | collective-permute-start | bytes 3145736 | tf_op jit(solution)/shard_map/ppermute | solution.py:44
  24.4 12.4 %collective-permute-start.6 = (bf16[2176,128]{1,0:T(8,128)(2,1)S(1)}, bf16[2176,128]{1,0:T(8,128)(2,1)S(1)}, u32[]{:S(2)}, u32[]{:S(2)}) collective-permute-start(bf16[2176,128]{1,0:T(8,128)(2,1)S(1)} %collective-permute-done.4.refs_7_), channel_id=1, source_target_pairs={{0,1},{1,0},{2,3},{3,2},{4,5},{5,4},{6,7},{7,6},{8,9},{9,8},{10,11... | collective-permute-start | bytes 1671176 | tf_op jit(solution)/shard_map/ppermute | solution.py:30
  24.4 12.4 %collective-permute-start.7 = (bf16[2176,128]{1,0:T(8,128)(2,1)S(1)}, bf16[2176,128]{1,0:T(8,128)(2,1)S(1)}, u32[]{:S(2)}, u32[]{:S(2)}) collective-permute-start(bf16[2176,128]{1,0:T(8,128)(2,1)S(1)} %collective-permute-done.5.refs_8_), channel_id=1, source_target_pairs={{0,1},{1,0},{2,3},{3,2},{4,5},{5,4},{6,7},{7,6},{8,9},{9,8},{10,11... | collective-permute-start | bytes 1671176 | tf_op jit(solution)/shard_map/ppermute | solution.py:30
  46.2 10.4 %collective-permute-start.10 = (bf16[528,128]{1,0:T(8,128)(2,1)S(1)}, bf16[528,128]{1,0:T(8,128)(2,1)S(1)}, u32[]{:S(2)}, u32[]{:S(2)}) collective-permute-start(bf16[528,128]{1,0:T(8,128)(2,1)S(1)} %get-tuple-element.61), channel_id=1, source_target_pairs={{0,192},{64,0},{128,64},{192,128},{1,193},{65,1},{129,65},{193,129... | collective-permute-start | bytes 405512 | tf_op jit(solution)/shard_map/ppermute | solution.py:30
  53.6 6.5 %collective-permute-start.11 = (bf16[528,128]{1,0:T(8,128)(2,1)S(1)}, bf16[528,128]{1,0:T(8,128)(2,1)S(1)}, u32[]{:S(2)}, u32[]{:S(2)}) collective-permute-start(bf16[528,128]{1,0:T(8,128)(2,1)S(1)} %get-tuple-element.62), channel_id=1, source_target_pairs={{0,64},{64,128},{128,192},{192,0},{1,65},{65,129},{129,193},{193,1... | collective-permute-start | bytes 405512 | tf_op jit(solution)/shard_map/ppermute | solution.py:30
  53.6 6.5 %collective-permute-start.12 = (bf16[528,128]{1,0:T(8,128)(2,1)S(1)}, bf16[528,128]{1,0:T(8,128)(2,1)S(1)}, u32[]{:S(2)}, u32[]{:S(2)}) collective-permute-start(bf16[528,128]{1,0:T(8,128)(2,1)S(1)} %get-tuple-element.63), channel_id=1, source_target_pairs={{0,128},{64,192},{128,0},{192,64},{1,129},{65,193},{129,1},{193,65... | collective-permute-start | bytes 405512 | tf_op jit(solution)/shard_map/ppermute | solution.py:30
  60.3 13.5 %collective-permute-start.17 = (bf16[512,1024]{1,0:T(8,128)(2,1)S(1)}, bf16[512,1024]{1,0:T(8,128)(2,1)S(1)}, u32[]{:S(2)}, u32[]{:S(2)}) collective-permute-start(bf16[512,1024]{1,0:T(8,128)(2,1)S(1)} %copy-done.4), channel_id=1, source_target_pairs={{0,1},{1,0},{2,3},{3,2},{4,5},{5,4},{6,7},{7,6},{8,9},{9,8},{10,11... | collective-permute-start | bytes 3145736 | tf_op jit(solution)/shard_map/ppermute | solution.py:30
  60.4 6.3 %collective-permute-start.26 = (bf16[128,512]{1,0:T(8,128)(2,1)S(1)}, bf16[128,512]{1,0:T(8,128)(2,1)S(1)}, u32[]{:S(2)}, u32[]{:S(2)}) collective-permute-start(bf16[128,512]{1,0:T(8,128)(2,1)S(1)} %merge.1), channel_id=1, source_target_pairs={{0,32},{2,34},{32,0},{34,2},{1,33},{3,35},{33,1},{35,3},{4,36},{6,... | collective-permute-start | bytes 393224 | tf_op jit(solution)/shard_map/ppermute | solution.py:30
  61.1 8.3 %collective-permute-start.27 = (bf16[128,512]{1,0:T(8,128)(2,1)S(1)}, bf16[128,512]{1,0:T(8,128)(2,1)S(1)}, u32[]{:S(2)}, u32[]{:S(2)}) collective-permute-start(bf16[128,512]{1,0:T(8,128)(2,1)S(1)} %merge.1), channel_id=1, source_target_pairs={{0,160},{32,128},{128,32},{160,0},{1,161},{33,129},{129,33},{161,1... | collective-permute-start | bytes 393224 | tf_op jit(solution)/shard_map/ppermute | solution.py:555
  63.5 9.7 %collective-permute-start.15 = (bf16[128,512]{1,0:T(8,128)(2,1)S(1)}, bf16[128,512]{1,0:T(8,128)(2,1)S(1)}, u32[]{:S(2)}, u32[]{:S(2)}) collective-permute-start(bf16[128,512]{1,0:T(8,128)(2,1)S(1)} %merge.1), channel_id=1, source_target_pairs={{0,128},{64,192},{128,0},{192,64},{1,129},{65,193},{129,1},{193,65... | collective-permute-start | bytes 393224 | tf_op jit(solution)/shard_map/ppermute | solution.py:30
  73.2 8.1 %collective-permute-start.16 = (bf16[256,512]{1,0:T(8,128)(2,1)S(1)}, bf16[256,512]{1,0:T(8,128)(2,1)S(1)}, u32[]{:S(2)}, u32[]{:S(2)}) collective-permute-start(bf16[256,512]{1,0:T(8,128)(2,1)S(1)} %constant_dynamic-update-slice_fusion.refs_0_), channel_id=1, source_target_pairs={{0,1},{1,0},{2,3},{3,2},{4,5},{5,4},{6,7},{7,6},{8,9},{9,8},{10,11... | collective-permute-start | bytes 786440 | tf_op jit(solution)/shard_map/ppermute | solution.py:30
  75.6 10.3 %collective-permute-start.33 = (bf16[16,2048]{1,0:T(8,128)(2,1)S(1)}, bf16[16,2048]{1,0:T(8,128)(2,1)S(1)}, u32[]{:S(2)}, u32[]{:S(2)}) collective-permute-start(bf16[16,2048]{1,0:T(8,128)(2,1)S(1)} %get-tuple-element.86), channel_id=1, source_target_pairs={{0,28},{4,0},{8,4},{12,8},{16,12},{20,16},{24,20},{28,24},{1,29},{... | collective-permute-start | bytes 196616 | tf_op jit(solution)/shard_map/ppermute | solution.py:30
  81.3 7.4 %collective-permute-start.29 = (bf16[16,2048]{1,0:T(8,128)(2,1)S(1)}, bf16[16,2048]{1,0:T(8,128)(2,1)S(1)}, u32[]{:S(2)}, u32[]{:S(2)}) collective-permute-start(bf16[16,2048]{1,0:T(8,128)(2,1)S(1)} %get-tuple-element.82), channel_id=1, source_target_pairs={{0,4},{4,8},{8,12},{12,16},{16,20},{20,24},{24,28},{28,0},{1,5},{5... | collective-permute-start | bytes 196616 | tf_op jit(solution)/shard_map/ppermute | solution.py:30
  85.9 5.8 %collective-permute-start.34 = (bf16[32,2048]{1,0:T(8,128)(2,1)S(1)}, bf16[32,2048]{1,0:T(8,128)(2,1)S(1)}, u32[]{:S(2)}, u32[]{:S(2)}) collective-permute-start(bf16[32,2048]{1,0:T(8,128)(2,1)S(1)} %pad_maximum_fusion.3), channel_id=1, source_target_pairs={{0,28},{4,0},{8,4},{12,8},{16,12},{20,16},{24,20},{28,24},{1,29},{... | collective-permute-start | bytes 393224 | tf_op jit(solution)/shard_map/ppermute | solution.py:30
  88.7 5.8 %collective-permute-start.30 = (bf16[32,2048]{1,0:T(8,128)(2,1)S(1)}, bf16[32,2048]{1,0:T(8,128)(2,1)S(1)}, u32[]{:S(2)}, u32[]{:S(2)}) collective-permute-start(bf16[32,2048]{1,0:T(8,128)(2,1)S(1)} %pad_maximum_fusion.2), channel_id=1, source_target_pairs={{0,4},{4,8},{8,12},{12,16},{16,20},{20,24},{24,28},{28,0},{1,5},{5... | collective-permute-start | bytes 393224 | tf_op jit(solution)/shard_map/ppermute | solution.py:30
  88.8 5.8 %collective-permute-start.23 = (bf16[32,2048]{1,0:T(8,128)(2,1)S(1)}, bf16[32,2048]{1,0:T(8,128)(2,1)S(1)}, u32[]{:S(2)}, u32[]{:S(2)}) collective-permute-start(bf16[32,2048]{1,0:T(8,128)(2,1)S(1)} %pad_maximum_fusion.1), channel_id=1, source_target_pairs={{0,28},{4,0},{8,4},{12,8},{16,12},{20,16},{24,20},{28,24},{1,29},{... | collective-permute-start | bytes 393224 | tf_op jit(solution)/shard_map/ppermute | solution.py:30
  91.6 5.8 %collective-permute-start.19 = (bf16[32,2048]{1,0:T(8,128)(2,1)S(1)}, bf16[32,2048]{1,0:T(8,128)(2,1)S(1)}, u32[]{:S(2)}, u32[]{:S(2)}) collective-permute-start(bf16[32,2048]{1,0:T(8,128)(2,1)S(1)} %pad_maximum_fusion), channel_id=1, source_target_pairs={{0,4},{4,8},{8,12},{12,16},{16,20},{20,24},{24,28},{28,0},{1,5},{5... | collective-permute-start | bytes 393224 | tf_op jit(solution)/shard_map/ppermute | solution.py:30
  94.5 6.1 %collective-permute-start.31 = (bf16[32,2048]{1,0:T(8,128)(2,1)S(1)}, bf16[32,2048]{1,0:T(8,128)(2,1)S(1)}, u32[]{:S(2)}, u32[]{:S(2)}) collective-permute-start(bf16[32,2048]{1,0:T(8,128)(2,1)S(1)} %add_convert_fusion.3), channel_id=1, source_target_pairs={{0,4},{4,8},{8,12},{12,16},{16,20},{20,24},{24,28},{28,0},{1,5},{5... | collective-permute-start | bytes 393224 | tf_op jit(solution)/shard_map/ppermute | solution.py:30
  94.7 6.0 %collective-permute-start.24 = (bf16[32,2048]{1,0:T(8,128)(2,1)S(1)}, bf16[32,2048]{1,0:T(8,128)(2,1)S(1)}, u32[]{:S(2)}, u32[]{:S(2)}) collective-permute-start(bf16[32,2048]{1,0:T(8,128)(2,1)S(1)} %add_convert_fusion.5), channel_id=1, source_target_pairs={{0,28},{4,0},{8,4},{12,8},{16,12},{20,16},{24,20},{28,24},{1,29},{... | collective-permute-start | bytes 393224 | tf_op jit(solution)/shard_map/ppermute | solution.py:30
  97.4 6.7 %collective-permute-start.20 = (bf16[32,2048]{1,0:T(8,128)(2,1)S(1)}, bf16[32,2048]{1,0:T(8,128)(2,1)S(1)}, u32[]{:S(2)}, u32[]{:S(2)}) collective-permute-start(bf16[32,2048]{1,0:T(8,128)(2,1)S(1)} %add_convert_fusion.7), channel_id=1, source_target_pairs={{0,4},{4,8},{8,12},{12,16},{16,20},{20,24},{24,28},{28,0},{1,5},{5... | collective-permute-start | bytes 393224 | tf_op jit(solution)/shard_map/ppermute | solution.py:30
  97.6 6.7 %collective-permute-start.36 = (bf16[32,2048]{1,0:T(8,128)(2,1)S(1)}, bf16[32,2048]{1,0:T(8,128)(2,1)S(1)}, u32[]{:S(2)}, u32[]{:S(2)}) collective-permute-start(bf16[32,2048]{1,0:T(8,128)(2,1)S(1)} %add_convert_fusion), channel_id=1, source_target_pairs={{0,28},{4,0},{8,4},{12,8},{16,12},{20,16},{24,20},{28,24},{1,29},{... | collective-permute-start | bytes 393224 | tf_op jit(solution)/shard_map/ppermute | solution.py:30
  100.6 6.1 %collective-permute-start.32 = (bf16[32,2048]{1,0:T(8,128)(2,1)S(1)}, bf16[32,2048]{1,0:T(8,128)(2,1)S(1)}, u32[]{:S(2)}, u32[]{:S(2)}) collective-permute-start(bf16[32,2048]{1,0:T(8,128)(2,1)S(1)} %add_convert_fusion.2), channel_id=1, source_target_pairs={{0,4},{4,8},{8,12},{12,16},{16,20},{20,24},{24,28},{28,0},{1,5},{5... | collective-permute-start | bytes 393224 | tf_op jit(solution)/shard_map/ppermute | solution.py:30
  100.8 5.9 %collective-permute-start.25 = (bf16[32,2048]{1,0:T(8,128)(2,1)S(1)}, bf16[32,2048]{1,0:T(8,128)(2,1)S(1)}, u32[]{:S(2)}, u32[]{:S(2)}) collective-permute-start(bf16[32,2048]{1,0:T(8,128)(2,1)S(1)} %add_convert_fusion.4), channel_id=1, source_target_pairs={{0,28},{4,0},{8,4},{12,8},{16,12},{20,16},{24,20},{28,24},{1,29},{... | collective-permute-start | bytes 393224 | tf_op jit(solution)/shard_map/ppermute | solution.py:30
  104.2 5.9 %collective-permute-start.21 = (bf16[32,2048]{1,0:T(8,128)(2,1)S(1)}, bf16[32,2048]{1,0:T(8,128)(2,1)S(1)}, u32[]{:S(2)}, u32[]{:S(2)}) collective-permute-start(bf16[32,2048]{1,0:T(8,128)(2,1)S(1)} %add_convert_fusion.6), channel_id=1, source_target_pairs={{0,4},{4,8},{8,12},{12,16},{16,20},{20,24},{24,28},{28,0},{1,5},{5... | collective-permute-start | bytes 393224 | tf_op jit(solution)/shard_map/ppermute | solution.py:30
  (10 other events, 142.3 us)
